TPU v7x, 256 devices: a whole 4x4x8 slice. The times are simulated.
256 devices in a mesh: dp: 128 (over y, z, x), tensor: 2 (over core).
Axes of the slice: x: 4, y: 4, z: 8, core: 2. Of those that a mesh axis runs over, the one named last changes fastest.
Arguments:
- layer_in: bfloat16 [98304, 1280], P('dp'), may hold values from -6 to 6
- ssm_in: bfloat16 [98304, 2560], P('dp', 'tensor'), may hold values from -6 to 6
- b_in: bfloat16 [98304, 128], P('dp'), may hold values from -1.5 to 1.5
- c_in: bfloat16 [98304, 128], P('dp'), may hold values from -1.5 to 1.5
- log_decay: float32 [98304, 40], P('dp', 'tensor'), may hold values from -1.5 to 0
- skip_gain: float32 [40], P('tensor'), may hold values from 0.5 to 1.5
- grad_out: bfloat16 [98304, 2560], P('dp', 'tensor'), may hold values from -6 to 6
- q_seed: int32 [1], replicated, may hold values from 0 to 46336
- error_in: bfloat16 [128, 1280, 2560], P('dp', None, 'tensor'), may hold values from -1.6 to 1.6
Outputs:
- grad_bc: float32 [98304, 256], P('dp')
- factor_p: float32 [64, 1280], P('tensor')
- factor_q: float32 [32, 2560], P(None, 'tensor')
- error_out: bfloat16 [128, 1280, 2560], P('dp', None, 'tensor')
All inputs are finite; a program needn't handle non-finite values.
Results may differ from a plain program's by a relative error of at most 0.0034.
The roundings to bfloat16 on the way count: a program that leaves them out, or rounds other values in their place, can miss the bound.
Values sent between devices are 32-bit elements; how exact they have to be, the bound alone decides.
A program may use at most 128 MiB of HBM per device.

v0:
```python
import jax
import jax.numpy as jnp
from jax import lax
from jax.sharding import PartitionSpec as P

SPAN = 256
R = 32


def start_factor(q_seed, rank_count, column_count, offset):
    rank_idx = lax.broadcasted_iota(jnp.int32, (rank_count, column_count), 0)
    column_idx = lax.broadcasted_iota(jnp.int32, (rank_count, column_count), 1) + offset
    section_one = (rank_idx * 7919 + column_idx * 104 + q_seed[0]) % 46337
    section_two = section_one * section_one % 46337
    section_three = (section_two * 211 + column_idx * 13 + rank_idx) % 46337
    section_four = section_three * section_three % 46337
    return section_four.astype(jnp.float32) * (2.0 / 46337.0) - 1.0


def scan_forward(inputs, log_decay, b_state, c_state, skip_gain, span_len):
    length_all, head_count, head_width = inputs.shape
    span_count = length_all // span_len
    blocked = inputs.reshape(span_count, span_len, head_count, head_width)
    decays = log_decay.reshape(span_count, span_len, head_count)
    b_blocks = b_state.reshape(span_count, span_len, -1)
    c_blocks = c_state.reshape(span_count, span_len, -1)
    cumulative = jnp.cumsum(decays, axis=1)
    causal = (
        lax.broadcasted_iota(jnp.int32, (span_len, span_len), 0)
        >= lax.broadcasted_iota(jnp.int32, (span_len, span_len), 1)
    )[None, :, :, None]
    gaps_log = cumulative[:, :, None, :] - cumulative[:, None, :, :]
    within = jnp.where(causal, jnp.exp(jnp.where(causal, gaps_log, 0.0)), 0.0)
    scores = jnp.einsum("ctn,csn->cts", c_blocks, b_blocks, precision=lax.Precision.HIGHEST)
    inside = jnp.einsum(
        "cts,ctsh,cshp->cthp", scores, within, blocked, precision=lax.Precision.HIGHEST
    )
    remain = jnp.exp(cumulative[:, -1:, :] - cumulative)
    states = jnp.einsum(
        "csh,cshp,csn->chpn", remain, blocked, b_blocks, precision=lax.Precision.HIGHEST
    )
    passing = jnp.exp(cumulative[:, -1, :])

    def advance(running, step_in):
        state_new, factor = step_in
        return (running * factor[:, None, None] + state_new, running)

    initial = jnp.zeros(states.shape[1:], jnp.float32)
    _, entering = lax.scan(advance, initial, (states, passing))
    carried = jnp.einsum(
        "cth,ctn,chpn->cthp",
        jnp.exp(cumulative),
        c_blocks,
        entering,
        precision=lax.Precision.HIGHEST,
    )
    result = inside + carried + skip_gain[None, None, :, None] * blocked
    return result.reshape(length_all, head_count * head_width)


def body(layer_in, ssm_in, b_in, c_in, log_decay, skip_gain, grad_out, q_seed, error_in):
    tok_rows = layer_in.shape[0]
    head_count = log_decay.shape[1]
    columns = ssm_in.shape[1]
    head_width = columns // head_count

    def forward(signal, b_state, c_state):
        return scan_forward(signal, log_decay, b_state, c_state, skip_gain, SPAN)

    _, pullback = jax.vjp(
        forward,
        ssm_in.astype(jnp.float32).reshape(tok_rows, head_count, head_width),
        b_in.astype(jnp.float32),
        c_in.astype(jnp.float32),
    )
    grad_signal, grad_b, grad_c = pullback(grad_out.astype(jnp.float32))
    grad_bc = lax.psum(jnp.concatenate([grad_b, grad_c], axis=1), "tensor")
    rounded = grad_signal.reshape(tok_rows, columns).astype(jnp.bfloat16)
    whole = (
        jnp.einsum("td,te->de", layer_in, rounded, preferred_element_type=jnp.float32) / tok_rows
    )
    whole = whole + error_in[0].astype(jnp.float32)
    start = start_factor(q_seed, R, columns, lax.axis_index("tensor") * columns)
    partial_p = jnp.einsum("re,de->rd", start, whole, precision=lax.Precision.HIGHEST)
    summed = lax.psum(partial_p, "dp")
    gram = jnp.einsum("rd,sd->rs", summed, summed, precision=lax.Precision.HIGHEST)
    lower = jnp.linalg.cholesky(gram)
    basis = jax.scipy.linalg.solve_triangular(lower, summed, lower=True)
    partial_q = jnp.einsum("rd,de->re", basis, whole, precision=lax.Precision.HIGHEST)
    summed_q = lax.psum(partial_q, "dp")
    correction = jnp.einsum(
        "rd,re->de", basis, summed_q, precision=lax.Precision.HIGHEST
    ) / lax.axis_size("dp")
    error_out = (whole - correction).astype(jnp.bfloat16)[None]
    return (grad_bc, basis, summed_q, error_out)


def solution(mesh):
    in_specs = (
        P("dp", None),
        P("dp", "tensor"),
        P("dp", None),
        P("dp", None),
        P("dp", "tensor"),
        P("tensor"),
        P("dp", "tensor"),
        P(),
        P("dp", None, "tensor"),
    )
    out_specs = (P("dp", None), P("tensor", None), P(None, "tensor"), P("dp", None, "tensor"))
    return jax.shard_map(body, mesh=mesh, in_specs=in_specs, out_specs=out_specs, check_vma=False)
```

profile of v0, /device:TPU:2, one launch (start us, length us, event | category | flops | bytes accessed | tf_op | source)
XLA Modules:
  0.0 585.6 jit_solution(10178374826362762844)
XLA Ops:
  7.2 1.0 reshape.65
  8.4 1.7 reduce-window.6
  12.0 6.6 %reshape.82 = bf16[3,256,20,64]{3,2,1,0:T(8,128)(2,1)} reshape(bf16[768,1280]{1,0:T(8,128)(2,1)} %param.14) | data formatting | bytes 3932160 | tf_op jit(solution)/shard_map/jvp()/reshape;reshape | solution.py:23
  18.7 6.2 %copy.40 = bf16[3,256,20,64]{1,3,2,0:T(8,128)(2,1)} copy(bf16[3,256,20,64]{3,2,1,0:T(8,128)(2,1)} %reshape.82) | data formatting | bytes 3932160 | tf_op jit(solution)/shard_map/jvp()/reshape;reshape | solution.py:23
  24.9 4.9 fusion.24
  29.7 1.6 broadcast.92.clone
  31.3 8.0 %while.32 = (s32[]{:T(128)}, f32[20,64,128]{2,1,0:T(8,128)S(1)}, f32[3,20,64,128]{3,2,1,0:T(8,128)}, f32[3,20,1,1]{1,3,2,0:T(1,128)}, f32[3,20]{1,0:T(4,128)S(1)...) while((s32[]{:T(128)}, f32[20,64,128]{2,1,0:T(8,128)S(1)}, f32[3,20,64,128]{3,2,1,0:T(8,128)}, ...), condition=%wide.region_3.4_spmd.clone, body=%wide.region_2.3_spmd.clone.sunk | while | flops 655363 | bytes 3277752 | solution.py:49
  31.3 0.9 bitcast_dynamic-update-slice_fusion.4
  32.2 1.2 bitcast_add_fusion.5
  34.0 0.9 bitcast_dynamic-update-slice_fusion.4
  34.9 1.2 bitcast_add_fusion.5
  36.7 0.9 bitcast_dynamic-update-slice_fusion.4
  37.6 1.2 bitcast_add_fusion.5
  39.3 3.9 copy.41
  43.3 6.4 %reshape.68 = bf16[3,256,20,64]{1,0,3,2:T(4,128)(2,1)} reshape(bf16[768,1280]{0,1:T(8,128)(2,1)} %copy.41) | data formatting | bytes 3932160 | tf_op jit(solution)/shard_map/transpose(jvp())/reshape | solution.py:58
  49.7 5.1 fusion.18
  54.8 1.5 broadcast.92
  56.3 8.3 %while.33 = (s32[]{:T(128)}, f32[20,64,128]{2,1,0:T(8,128)S(1)}, f32[3,20,64,128]{3,2,1,0:T(8,128)}, f32[3,20,64,128]{3,2,1,0:T(8,128)}, f32[3,20,1,1]{1,3,2,0:T(1,128)}, /*index=5*/s32[]{:T(128)}, s32[]{:T(128)}, s32[]{:T(128)}) while((s32[]{:T(128)}, f32[20,64,128]{2,1,0:T(8,128)S(1)}, f32[3,20,64,128]{3,2,1,0:T(8,128)}, ...), condition=%wide.region_5.6_spmd.clone, body=%wide.region_4.5_spmd.clone.sunk | while | flops 655364 | bytes 3277168 | solution.py:49
  56.3 0.9 bitcast_dynamic-update-slice_fusion.5
  57.8 1.2 bitcast_add_fusion.6
  59.1 0.9 bitcast_dynamic-update-slice_fusion.5
  60.6 1.2 bitcast_add_fusion.6
  61.8 0.9 bitcast_dynamic-update-slice_fusion.5
  63.4 1.2 bitcast_add_fusion.6
  64.7 3.4 fusion.88
  68.4 11.0 %fusion.22 = bf16[3,256,20,64]{1,3,2,0:T(8,128)(2,1)S(1)} fusion(f32[3,20,64,256]{3,2,1,0:T(8,128)S(1)} %fusion.88, f32[3,256,256]{2,1,0:T(8,128)S(1)} %fusion.89, f32[3,256,20]{1,2,0:T(8,128)S(1)} %bitcast.135, pred[256,256]{1,0:T(8,128)(4,1)S(1)} %copy-done.15, f32[20]{0:T(128)S(1)} %copy-done.16, f32[3,256,20]{1,2,0:T(8,128)S(1)} %get-tuple-element.217, ...), kind=kOutput, calls=%fused_computation.33 | convolution fusion | flops 3041525760 | bytes 10805328 | tf_op jit(solution)/shard_map/transpose(jvp(cts,ctsh,cshp->cthp))/dot_general | solution.py:35
  79.4 1.7 copy.47
  81.2 1.8 copy.66
  83.0 5.6 copy.48
  89.3 5.3 fusion.7
  94.6 2.7 copy-done.1
  97.3 4.8 fusion.50
  102.2 7.6 %fusion.2 = f32[3,256,256]{2,1,0:T(8,128)S(1)} fusion(f32[3,256,20]{1,2,0:T(8,128)S(1)} %bitcast.136, pred[256,256]{1,0:T(8,128)(4,1)S(1)} %copy-done.15, bf16[3,256,20,64]{1,3,2,0:T(8,128)(2,1)} %copy.40, bf16[3,20,256,64]{2,0,3,1:T(4,128)(2,1)} %bitcast.122), kind=kOutput, calls=%fused_computation.10 | convolution fusion | flops 522780672 | bytes 4845568 | tf_op jit(solution)/shard_map/transpose(jvp(cts,ctsh,cshp->cthp))/dot_general | solution.py:35
  109.9 7.1 %fusion.33 = f32[3,256,128]{2,1,0:T(8,128)} fusion(f32[3,20,64,128]{3,2,1,0:T(8,128)S(1)} %copy-done.3, bf16[3,256,20,64]{1,3,2,0:T(8,128)(2,1)S(1)} %copy-done.2, f32[3,256,20]{1,2,0:T(8,128)S(1)} %get-tuple-element.217), kind=kOutput, calls=%fused_computation.44 | convolution fusion | flops 1511915520 | bytes 4386816 | tf_op jit(solution)/shard_map/transpose(jvp(csh,cshp,csn->chpn))/dot_general | solution.py:39
  117.0 6.5 %fusion.34 = f32[3,256,128]{2,1,0:T(8,128)S(1)} fusion(f32[3,20,64,128]{3,2,1,0:T(8,128)S(1)} %copy-done.7, f32[3,256,20]{1,2,0:T(8,128)S(1)} %copy-done.14, bf16[3,256,20,64]{1,0,3,2:T(4,128)(2,1)S(1)} %copy-done.5), kind=kOutput, calls=%fused_computation.45 | convolution fusion | flops 1511915520 | bytes 4386816 | tf_op jit(solution)/shard_map/transpose(jvp(cth,ctn,chpn->cthp))/dot_general | solution.py:50
  123.5 1.2 convolution_add_fusion
  124.7 191.0 %all-reduce.6.cloned.1.call-done = f32[32,1280]{1,0:T(8,128)} async-done(((f32[32,1280]{1,0:T(8,128)}), f32[32,1280]{1,0:T(8,128)}) %all-reduce.6.cloned.1.call-update) | async-done | bytes 163856 | tf_op jit(solution)/shard_map/psum | solution.py:85
  315.8 1.3 fusion.90
  317.1 2.9 cholesky.16
  321.4 2.4 custom-call.7
  323.8 1.3 fusion.77
  325.1 9.5 %fusion.91 = f32[32,1280]{1,0:T(8,128)} fusion(f32[32,1280]{1,0:T(8,128)S(1)} %fusion.77, f32[1280,1280]{0,1:T(8,128)} %copy-done.1), kind=kOutput, calls=%fused_computation.118 | convolution fusion | flops 629145600 | bytes 6881280 | tf_op jit(solution)/shard_map/rd,de->re/dot_general | solution.py:89
  335.6 1.9 pad_maximum_fusion
  337.5 206.6 %all-reduce.8.cloned.1.call-done = f32[32,1280]{1,0:T(8,128)} async-done(((f32[32,1280]{1,0:T(8,128)}), f32[32,1280]{1,0:T(8,128)}) %all-reduce.8.cloned.1.call-update) | async-done | bytes 163856 | tf_op jit(solution)/shard_map/psum | solution.py:90
  544.1 9.0 %fusion.14 = bf16[1,1280,1280]{1,2,0:T(8,128)(2,1)} fusion(f32[1280,1280]{0,1:T(8,128)} %copy-done.1, f32[32,1280]{1,0:T(8,128)S(1)} %fusion.77, f32[32,1280]{1,0:T(8,128)} %all-reduce.8.cloned.1.call-done), kind=kOutput, calls=%fused_computation.25 | convolution fusion | flops 634060800 | bytes 10158080 | tf_op jit(solution)/shard_map/rd,re->de/dot_general | solution.py:91
  553.1 5.9 %copy.51 = bf16[1,1280,1280]{2,1,0:T(8,128)(2,1)} copy(bf16[1,1280,1280]{1,2,0:T(8,128)(2,1)} %fusion.14) | data formatting | bytes 6553600
  559.0 17.1 %all-reduce.4.cloned.1.call-done = f32[768,256]{1,0:T(8,128)} async-done(((f32[768,256]{1,0:T(8,128)}), f32[768,256]{1,0:T(8,128)}) %all-reduce.4.cloned.1.call-update) | async-done | bytes 786448 | tf_op jit(solution)/shard_map/psum | solution.py:77
  576.1 2.1 copy.110
  (73 shorter events, 9.0 us)
Async XLA Ops:
  7.2 82.1 %copy-start = (bf16[768,1280]{1,0:T(8,128)(2,1)S(1)}, bf16[768,1280]{1,0:T(8,128)(2,1)}, u32[]{:S(2)}) copy-start(bf16[768,1280]{1,0:T(8,128)(2,1)} %param.13) | copy-start | bytes 5898244
  7.2 308.6 %all-reduce.6.cloned.1.call-start = ((), (), s32[]{:S(2)}) async-start(), calls=%async_computation.1 | async-start | bytes 327680 | tf_op jit(solution)/shard_map/psum | solution.py:85
  10.5 1.5 copy-start.12
  18.7 6.2 %copy-start.6 = (bf16[768,128]{1,0:T(8,128)(2,1)S(1)}, bf16[768,128]{1,0:T(8,128)(2,1)}, u32[]{:S(2)}) copy-start(bf16[768,128]{1,0:T(8,128)(2,1)} %param.15) | copy-start | bytes 589828
  43.3 6.4 %copy-start.8 = (bf16[768,128]{1,0:T(8,128)(2,1)S(1)}, bf16[768,128]{1,0:T(8,128)(2,1)}, u32[]{:S(2)}) copy-start(bf16[768,128]{1,0:T(8,128)(2,1)} %param.16) | copy-start | bytes 589828
  43.3 6.4 %copy-start.14 = (f32[3,256,20]{1,2,0:T(8,128)S(1)}, f32[3,256,20]{1,2,0:T(8,128)}, u32[]{:S(2)}) copy-start(f32[3,256,20]{1,2,0:T(8,128)} %get-tuple-element.216) | copy-start | bytes 184324
  64.6 3.7 copy-start.4
  64.6 3.7 copy-start.13
  64.7 3.7 copy-start.15
  64.7 3.7 copy-start.16
  94.6 2.7 copy-start.1
  102.2 441.9 %all-reduce.8.cloned.1.call-start = ((), (), s32[]{:S(2)}) async-start(), calls=%async_computation.2 | async-start | bytes 327680 | tf_op jit(solution)/shard_map/psum | solution.py:90
  102.2 7.6 %copy-start.2 = (bf16[3,256,20,64]{1,3,2,0:T(8,128)(2,1)S(1)}, bf16[3,256,20,64]{1,3,2,0:T(8,128)(2,1)}, u32[]{:S(2)}) copy-start(bf16[3,256,20,64]{1,3,2,0:T(8,128)(2,1)} %copy.40) | copy-start | bytes 5898244
  102.2 7.6 %copy-start.3 = (f32[3,20,64,128]{3,2,1,0:T(8,128)S(1)}, f32[3,20,64,128]{3,2,1,0:T(8,128)}, u32[]{:S(2)}) copy-start(f32[3,20,64,128]{3,2,1,0:T(8,128)} %get-tuple-element.141) | copy-start | bytes 5898244
  102.2 14.7 %copy-start.7 = (f32[3,20,64,128]{3,2,1,0:T(8,128)S(1)}, f32[3,20,64,128]{3,2,1,0:T(8,128)}, u32[]{:S(2)}) copy-start(f32[3,20,64,128]{3,2,1,0:T(8,128)} %get-tuple-element.142) | copy-start | bytes 5898244
  109.9 7.1 %copy-start.5 = (bf16[3,256,20,64]{1,0,3,2:T(4,128)(2,1)S(1)}, bf16[3,256,20,64]{1,0,3,2:T(4,128)(2,1)}, u32[]{:S(2)}) copy-start(bf16[3,256,20,64]{1,0,3,2:T(4,128)(2,1)} %reshape.68) | copy-start | bytes 5898244
  325.1 219.0 %copy-start.10 = (f32[32,1280]{1,0:T(8,128)}, f32[32,1280]{1,0:T(8,128)S(1)}, u32[]{:S(2)}) copy-start(f32[32,1280]{1,0:T(8,128)S(1)} %fusion.77) | copy-start | bytes 491524
  325.1 9.6 %copy-start.9 = (f32[3,256,128]{2,1,0:T(8,128)S(1)}, f32[3,256,128]{2,1,0:T(8,128)}, u32[]{:S(2)}) copy-start(f32[3,256,128]{2,1,0:T(8,128)} %fusion.33) | copy-start | bytes 1179652
  334.6 241.5 %all-reduce.4.cloned.1.call-start = ((), (), s32[]{:S(2)}) async-start(), calls=%async_computation | async-start | bytes 1572864 | tf_op jit(solution)/shard_map/psum | solution.py:77
  553.1 25.0 %copy-start.11 = (f32[32,1280]{1,0:T(8,128)S(1)}, f32[32,1280]{1,0:T(8,128)}, u32[]{:S(2)}) copy-start(f32[32,1280]{1,0:T(8,128)} %all-reduce.8.cloned.1.call-done) | copy-start | bytes 491524
Sparse Core Ops, SparseCore 0:
  102.3 213.4 all-reduce.5
  334.8 209.2 all-reduce.7
  547.3 28.7 all-reduce.3
where the time goes:
time: 595 us; the launch traced here: 586 us
  waiting for transfers between devices  415 us (70%)
  matrix products  79.1 us (13%)
  local copies, waits for them, and re-layouts  52 us (9%)
  other arithmetic  24.5 us (4%)
  between operations  15 us (3%)
    psum x1, waiting for transfers between devices, body(): summed_q = lax.psum(partial_q, 'dp')  207 us
    psum x1, waiting for transfers between devices, body(): summed = lax.psum(partial_p, 'dp')  191 us
    unnamed x40, local copies, waits for them, and re-layouts  22.8 us
    dot_general x2, matrix products, scan_forward(): jnp.einsum('cts,ctsh,cshp->cthp', scores, within, blocked, precision=lax....  18.6 us
    psum x1, waiting for transfers between devices, body(): grad_bc = lax.psum(jnp.concatenate([grad_b, grad_c], axis=1), 'tensor')  17.1 us
    dot_general x3, matrix products, scan_forward(): jnp.einsum('csh,cshp,csn->chpn', remain, blocked, b_blocks, precision=lax...  15.3 us
    another operation x2, local copies, waits for them, and re-layouts, scan_forward(): blocked = inputs.reshape(span_count, span_len, head_count, head_width)  12.8 us
  transfers between devices with their start and end apart: 3, of which 3 were waited for; matrix products, arithmetic and copies ran while one was open for 7% of the time, Pallas kernels for 0%

commit v1 on v0

v1 whole, which is shorter than its diff:
```python
import jax
import jax.numpy as jnp
from jax import lax
from jax.experimental import pallas as pl
from jax.experimental.pallas import tpu as pltpu
from jax.sharding import PartitionSpec as P

R = 32
TOK = 768
D = 1280
COLS = 1280
HEADS = 20
N = 128
BLK = 128
NB = TOK // BLK
PAIRS = HEADS // 2
NX, NY, NZ = 4, 4, 8
PR, PC = 8, 384
WIDE = NY * PC
ROWS = 256
F32 = jnp.float32
BF16 = jnp.bfloat16
MESH = pl.DeviceIdType.MESH
VMEM = pltpu.VMEM

NN = (((1,), (0,)), ((), ()))
NT = (((1,), (1,)), ((), ()))
TN = (((0,), (0,)), ((), ()))


def mm(a, b, dims=NN):
    return lax.dot_general(a, b, dims, preferred_element_type=F32)


def split2(v):
    hi = v.astype(BF16)
    lo = (v - hi.astype(F32)).astype(BF16)
    return hi, lo


def split3(v):
    hi = v.astype(BF16)
    rest = v - hi.astype(F32)
    mid = rest.astype(BF16)
    lo = (rest - mid.astype(F32)).astype(BF16)
    return hi, mid, lo


def iota(shape, dim):
    return lax.broadcasted_iota(jnp.int32, shape, dim)


def scan_kernel(
    x_ref, dy_ref, b_ref, c_ref, ld_ref, gain_ref,
    gx_ref, gbc_ref,
    ldp, cum, cum_t, gainp, gain_row, remain, xs, dys, entering, grad_state, passing,
):
    ldp[...] = jnp.zeros((TOK, 128), F32)
    ldp[:, 0:HEADS] = ld_ref[...]
    gainp[...] = jnp.zeros((8, 128), F32)
    gainp[0:1, 0:HEADS] = gain_ref[...]
    expand = (iota((128, COLS), 0) == iota((128, COLS), 1) // 64).astype(BF16)
    expand2 = jnp.concatenate([expand, expand], axis=0)
    gain_hi, gain_mid, gain_lo = split3(gainp[...])
    gain_row[...] = mm(gain_hi, expand) + mm(gain_mid, expand) + mm(gain_lo, expand)
    lower = (iota((BLK, BLK), 0) >= iota((BLK, BLK), 1)).astype(BF16)
    lower3 = jnp.concatenate([lower, lower, lower], axis=1)

    state = jnp.zeros((N, COLS), F32)
    for c in range(NB):
        rows = pl.ds(c * BLK, BLK)
        parts = jnp.concatenate(split3(ldp[rows, :]), axis=0)
        total = mm(lower3, parts)
        cum[rows, :] = total
        cum_t[rows, :] = total.T
        factors = jnp.concatenate([jnp.exp(total), jnp.exp(total[BLK - 1 : BLK, :] - total)], axis=0)
        factors2 = jnp.concatenate(split2(factors), axis=1)
        wide = mm(factors2, expand2)
        grow, left = wide[:BLK], wide[BLK:]
        remain[rows, :] = left
        passing[8 * c : 8 * c + 8, :] = grow[BLK - 8 : BLK]
        x_scaled = (x_ref[rows, :].astype(F32) * left).astype(BF16)
        dy_scaled, dy_rest = split2(dy_ref[rows, :].astype(F32) * grow)
        xs[rows, :] = x_scaled
        dys[rows, :] = dy_scaled
        entering[rows, :] = state.astype(BF16)
        if c < NB - 1:
            state = state * grow[BLK - 1 : BLK] + mm(b_ref[rows, :], x_scaled, TN)
        if c > 0:
            c_blk = c_ref[rows, :]
            grad_state[rows, :] = mm(
                jnp.concatenate([c_blk, c_blk], axis=0), jnp.concatenate([dy_scaled, dy_rest], axis=0), TN
            )

    causal = iota((BLK, BLK), 0) <= iota((BLK, BLK), 1)
    causal2 = jnp.concatenate([causal, causal], axis=1)
    low_half = iota((BLK, 128), 1) < 64
    after = jnp.zeros((N, COLS), F32)
    for c in range(NB - 1, -1, -1):
        rows = pl.ds(c * BLK, BLK)
        b_blk, c_blk = b_ref[rows, :], c_ref[rows, :]
        if c < NB - 1:
            after16, after_rest = split2(after)
            carried = mm(jnp.concatenate([b_blk, b_blk], axis=1), jnp.concatenate([after16, after_rest], axis=0))
            carried = carried * remain[rows, :]
            grad_b = mm(xs[rows, :], after16, NT)
        scores = mm(b_blk, c_blk, NT)
        scores2 = jnp.concatenate([scores, scores], axis=1)
        gaps = jnp.zeros((BLK, BLK), F32)
        for j in range(PAIRS):
            lanes = slice(128 * j, 128 * j + 128)
            dy_pair = dy_ref[rows, lanes]
            zero = jnp.zeros_like(dy_pair)
            both = jnp.concatenate(
                [jnp.where(low_half, dy_pair, zero), jnp.where(low_half, zero, dy_pair)], axis=0
            )
            h = 2 * j
            to_row = jnp.concatenate(
                [cum_t[c * BLK + h : c * BLK + h + 1, :], cum_t[c * BLK + h + 1 : c * BLK + h + 2, :]],
                axis=1,
            )
            from_col = jnp.concatenate(
                [
                    jnp.broadcast_to(cum[rows, h : h + 1], (BLK, BLK)),
                    jnp.broadcast_to(cum[rows, h + 1 : h + 2], (BLK, BLK)),
                ],
                axis=1,
            )
            decay = jnp.exp(jnp.where(causal2, to_row - from_col, -1e30))
            weights, weights_rest = split2(decay * scores2)
            grad_x = mm(weights, both) + mm(weights_rest, both) + gain_row[0:1, lanes] * dy_pair.astype(F32)
            if c < NB - 1:
                grad_x = grad_x + carried[:, lanes]
            gx_ref[rows, lanes] = grad_x.astype(BF16)
            products = mm(x_ref[rows, lanes], both, NT) * decay
            gaps = gaps + products[:, :BLK] + products[:, BLK:]
        gap_hi, gap_lo = split2(gaps)
        grad_b_in = mm(gap_hi, c_blk) + mm(gap_lo, c_blk)
        grad_c = mm(gap_hi, b_blk, TN) + mm(gap_lo, b_blk, TN)
        if c < NB - 1:
            grad_b_in = grad_b_in + grad_b
        if c > 0:
            grad_c = grad_c + mm(dys[rows, :], entering[rows, :], NT)
        gbc_ref[rows, 0:N] = grad_b_in
        gbc_ref[rows, N : 2 * N] = grad_c
        if c > 0:
            after = after * passing[8 * c + 7 : 8 * c + 8, :] + grad_state[rows, :]


def scan_backward(x, dy, b, c, ld, gain):
    vm = pl.BlockSpec(memory_space=VMEM)
    return pl.pallas_call(
        scan_kernel,
        out_shape=(
            jax.ShapeDtypeStruct((TOK, COLS), BF16),
            jax.ShapeDtypeStruct((TOK, 2 * N), F32),
        ),
        in_specs=[vm] * 6,
        out_specs=[vm] * 2,
        scratch_shapes=[
            VMEM((TOK, 128), F32),
            VMEM((TOK, 128), F32),
            VMEM((TOK, 128), F32),
            VMEM((8, 128), F32),
            VMEM((8, COLS), F32),
            VMEM((TOK, COLS), F32),
            VMEM((TOK, COLS), BF16),
            VMEM((TOK, COLS), BF16),
            VMEM((TOK, COLS), BF16),
            VMEM((TOK, COLS), F32),
            VMEM((8 * NB, COLS), F32),
        ],
        compiler_params=pltpu.CompilerParams(vmem_limit_bytes=48 * 1024 * 1024),
        cost_estimate=pl.CostEstimate(
            flops=2 * TOK * COLS * 1024, bytes_accessed=8_000_000, transcendentals=TOK * BLK * HEADS
        ),
    )(x, dy, b, c, ld, gain)


def mod(a):
    quotient = (a.astype(F32) * (1.0 / 46337.0)).astype(jnp.int32)
    left = a - quotient * 46337
    left = jnp.where(left < 0, left + 46337, left)
    return jnp.where(left >= 46337, left - 46337, left)


def start_factor(seed, offset):
    rank = iota((R, COLS), 0)
    column = iota((R, COLS), 1) + offset
    one = mod(rank * 7919 + column * 104 + seed)
    two = mod(one * one)
    three = mod(two * 211 + column * 13 + rank)
    four = mod(three * three)
    return four.astype(F32) * (2.0 / 46337.0) - 1.0


def fold3(v):
    return v[0:R] + v[R : 2 * R] + v[2 * R : 3 * R]


def stack3(v):
    return jnp.concatenate(split3(v), axis=0)


def inverse_factor(gram):
    work = jnp.concatenate(
        [gram, (iota((R, R), 0) == iota((R, R), 1)).astype(F32), jnp.zeros((R, 128 - 2 * R), F32)], axis=1
    )
    row_at = iota((R, 128), 0)
    diag = jnp.ones((R, 128), F32)
    for k in range(R):
        column = jnp.broadcast_to(work[:, k : k + 1], (R, 128))
        pivot = column[k : k + 1, :]
        diag = jnp.where(row_at == k, pivot, diag)
        scaled = work[k : k + 1, :] / pivot
        work = work - jnp.where(row_at > k, column, 0.0) * scaled
    return (work * lax.rsqrt(diag))[:, R : 2 * R]


class Comm:
    def __init__(self, local, full, slots, line, sems):
        self.local, self.full, self.slots, self.line, self.sems = local, full, slots, line, sems
        at = lax.axis_index("dp")
        self.core = lax.axis_index("tensor")
        self.x = lax.rem(at, NX)
        self.z = lax.rem(at // NX, NZ)
        self.y = at // (NX * NZ)

    def device(self, y, z, x):
        return ((y * NZ + z) * NX + x, self.core)

    def neighbour(self, k):
        return lax.rem(self.y + k // NX, NY), lax.rem(self.x + k % NX, NX)

    def piece(self, ref, y, x):
        return ref.at[pl.ds(pl.multiple_of(x * PR, PR), PR), pl.ds(pl.multiple_of(y * PC, 128), PC)]

    def scatter(self, k):
        y, x = self.neighbour(k)
        return pltpu.make_async_remote_copy(
            src_ref=self.piece(self.local, y, x),
            dst_ref=self.slots.at[k],
            send_sem=self.sems.at[0, k],
            recv_sem=self.sems.at[1, k],
            device_id=self.device(y, self.z, x),
            device_id_type=MESH,
        )

    def along(self, k):
        return pltpu.make_async_remote_copy(
            src_ref=self.line.at[self.z],
            dst_ref=self.line.at[self.z],
            send_sem=self.sems.at[2, k],
            recv_sem=self.sems.at[3, k],
            device_id=self.device(self.y, lax.rem(self.z + k, NZ), self.x),
            device_id_type=MESH,
        )

    def gather(self, k):
        y, x = self.neighbour(k)
        mine = self.piece(self.full, self.y, self.x)
        return pltpu.make_async_remote_copy(
            src_ref=mine,
            dst_ref=mine,
            send_sem=self.sems.at[4, k],
            recv_sem=self.sems.at[5, k],
            device_id=self.device(y, self.z, x),
            device_id_type=MESH,
        )

    def begin(self):
        for k in range(1, NX * NY):
            self.scatter(k).start()

    def middle(self):
        total = self.piece(self.local, self.y, self.x)[...]
        for k in range(1, NX * NY):
            self.scatter(k).wait_recv()
            total = total + self.slots[k]
        self.line[self.z] = total
        for k in range(1, NZ):
            self.along(k).start()

    def last(self):
        for k in range(1, NZ):
            self.along(k).wait_recv()
        total = self.line[0]
        for k in range(1, NZ):
            total = total + self.line[k]
        self.piece(self.full, self.y, self.x)[...] = total
        for k in range(1, NX * NY):
            self.gather(k).start()

    def end(self):
        for k in range(1, NX * NY):
            self.gather(k).wait_recv()

    def settle(self):
        for k in range(1, NX * NY):
            self.scatter(k).wait_send()
            self.gather(k).wait_send()
        for k in range(1, NZ):
            self.along(k).wait_send()


def compress_kernel(
    seed_ref, feat_ref, gx_ref, err_ref, gbc_ref,
    gbc_out, p_out, q_out, err_out,
    whole, done, other, local_p, full_p, slots_p, line_p, local_q, full_q, slots_q, line_q,
    sems_p, sems_q, pair_sems, out_sems,
):
    first = Comm(local_p, full_p, slots_p, line_p, sems_p)
    second = Comm(local_q, full_q, slots_q, line_q, sems_q)
    core = first.core
    at = lax.axis_index("dp")

    barrier = pltpu.get_barrier_semaphore()
    for k in range(1, NX * NY):
        y, x = first.neighbour(k)
        pl.semaphore_signal(barrier, inc=1, device_id=first.device(y, first.z, x), device_id_type=MESH)
    for k in range(1, NZ):
        pl.semaphore_signal(
            barrier, inc=1, device_id=first.device(first.y, lax.rem(first.z + k, NZ), first.x), device_id_type=MESH
        )
    pl.semaphore_signal(barrier, inc=1, device_id=(at, 1 - core), device_id_type=MESH)

    local_p[:, D:] = jnp.zeros((R, WIDE - D), F32)
    local_q[:, D:] = jnp.zeros((R, WIDE - D), F32)
    start = stack3(start_factor(seed_ref[0], core * COLS))
    through = fold3(mm(start, gx_ref[...], NT))
    own = mm(stack3(through), feat_ref[...]) * (1.0 / TOK) + mm(start, err_ref[...], NT)
    local_p[:, :D] = fold3(own)

    pl.semaphore_wait(barrier, NX * NY - 1 + NZ - 1 + 1)
    first.begin()
    swap = pltpu.make_async_remote_copy(
        src_ref=gbc_ref,
        dst_ref=other,
        send_sem=pair_sems.at[0],
        recv_sem=pair_sems.at[1],
        device_id=(at, 1 - core),
        device_id_type=MESH,
    )
    swap.start()

    def whole_rows(i):
        rows = pl.ds(i * ROWS, ROWS)
        part = mm(feat_ref[:, i * ROWS : (i + 1) * ROWS], gx_ref[...], TN)
        whole[rows, :] = part * (1.0 / TOK) + err_ref[rows, :].astype(F32)

    whole_rows(0)
    first.middle()
    whole_rows(1)
    first.last()
    whole_rows(2)
    first.end()

    psum = full_p[:, :D]
    parts = stack3(psum)
    cross = mm(parts, parts, NT)
    gram = jnp.zeros((R, R), F32)
    for a in range(2, -1, -1):
        for b in range(2, -1, -1):
            gram = gram + cross[R * a : R * a + R, R * b : R * b + R]
    inverse = inverse_factor(gram)
    basis = lax.dot_general(inverse, psum, NN, precision=lax.Precision.HIGHEST, preferred_element_type=F32)
    p_out[...] = basis
    basis3 = stack3(basis)
    through = fold3(mm(basis3, feat_ref[...], NT))
    own = mm(stack3(through), gx_ref[...]) * (1.0 / TOK) + mm(basis3, err_ref[...])
    local_q[:, :COLS] = fold3(own)

    second.begin()
    whole_rows(3)
    second.middle()
    whole_rows(4)
    second.last()
    swap.wait()
    gbc_out[...] = gbc_ref[...] + other[...]
    second.end()

    summed = full_q[:, :COLS]
    q_out[...] = summed
    q_hi, q_lo = split2(summed)
    p_hi, p_lo = split2(basis * (1.0 / 128.0))
    left = jnp.concatenate([p_hi, p_hi, p_lo, p_lo], axis=0)
    right = jnp.concatenate([q_hi, q_lo, q_hi, q_lo], axis=0)
    copies = []
    for i in range(D // ROWS):
        rows = pl.ds(i * ROWS, ROWS)
        correction = mm(left[:, i * ROWS : (i + 1) * ROWS], right, TN)
        done[rows, :] = (whole[rows, :] - correction).astype(BF16)
        copy = pltpu.make_async_copy(done.at[rows, :], err_out.at[0, rows, :], out_sems.at[i])
        copy.start()
        copies.append(copy)
    first.settle()
    second.settle()
    for copy in copies:
        copy.wait()


def compress(seed, feat, gx, err, gbc):
    vm = pl.BlockSpec(memory_space=VMEM)
    piece = VMEM((R, WIDE), F32)
    slots = VMEM((NX * NY, PR, PC), F32)
    line = VMEM((NZ, PR, PC), F32)
    return pl.pallas_call(
        compress_kernel,
        out_shape=(
            jax.ShapeDtypeStruct((TOK, 2 * N), F32),
            jax.ShapeDtypeStruct((R, D), F32),
            jax.ShapeDtypeStruct((R, COLS), F32),
            jax.ShapeDtypeStruct((1, D, COLS), BF16),
        ),
        in_specs=[pl.BlockSpec(memory_space=pltpu.SMEM), vm, vm, vm, vm],
        out_specs=[vm, vm, vm, pl.BlockSpec(memory_space=pl.ANY)],
        scratch_shapes=[
            VMEM((D, COLS), F32),
            VMEM((D, COLS), BF16),
            VMEM((TOK, 2 * N), F32),
            piece, piece, slots, line,
            piece, piece, slots, line,
            pltpu.SemaphoreType.DMA((6, NX * NY)),
            pltpu.SemaphoreType.DMA((6, NX * NY)),
            pltpu.SemaphoreType.DMA((2,)),
            pltpu.SemaphoreType.DMA((D // ROWS,)),
        ],
        compiler_params=pltpu.CompilerParams(
            collective_id=0, has_side_effects=True, vmem_limit_bytes=48 * 1024 * 1024
        ),
        cost_estimate=pl.CostEstimate(
            flops=2 * D * COLS * 1100, bytes_accessed=14_000_000, transcendentals=0
        ),
    )(seed, feat, gx, err, gbc)


def body(layer_in, ssm_in, b_in, c_in, log_decay, skip_gain, grad_out, q_seed, error_in):
    gx, gbc = scan_backward(ssm_in, grad_out, b_in, c_in, log_decay, skip_gain.reshape(1, HEADS))
    return compress(q_seed, layer_in, gx, error_in.reshape(D, COLS), gbc)


def solution(mesh):
    in_specs = (
        P("dp", None),
        P("dp", "tensor"),
        P("dp", None),
        P("dp", None),
        P("dp", "tensor"),
        P("tensor"),
        P("dp", "tensor"),
        P(),
        P("dp", None, "tensor"),
    )
    out_specs = (P("dp", None), P("tensor", None), P(None, "tensor"), P("dp", None, "tensor"))
    return jax.shard_map(body, mesh=mesh, in_specs=in_specs, out_specs=out_specs, check_vma=False)
```

time: 595 us -> 76.5 us (0.13); the launches traced: 586 us -> 75.9 us
  waiting for transfers between devices: 415 us -> 0 us
  matrix products: 79.1 us -> 0 us
  Pallas kernels: 0 us -> 63.4 us
  local copies, waits for them, and re-layouts: 52 us -> 11.2 us
  other arithmetic: 24.5 us -> 0 us
  between operations: 15 us -> 1.31 us
    psum x3 -> x0, waiting for transfers between devices: 415 us -> none  [the longest x1 207 us: body(): summed_q = lax.psum(partial_q, 'dp')]
    dot_general x15 -> x0, matrix products: 77.8 us -> none  [the longest x2 18.6 us: scan_forward(): jnp.einsum('cts,ctsh,cshp->cthp', scores, within, blocked, precision=lax....]
    pallas_call x0 -> x2, Pallas kernels: none -> 63.4 us  [the longest x1 51 us: compress(): pl.pallas_call(compress_kernel, out_shape=(jax.ShapeDtypeStruct((TOK, 2 *...]
    another operation x10 -> x0, local copies, waits for them, and re-layouts: 16.2 us -> none  [the longest x2 12.8 us: scan_forward(): blocked = inputs.reshape(span_count, span_len, head_count, head_width)]
    unnamed x40 -> x15, local copies, waits for them, and re-layouts: 22.8 us -> 11.2 us
    another operation x8 -> x0, other arithmetic: 8.55 us -> none  [the longest x3 3.6 us: body(): lower = jnp.linalg.cholesky(gram)]
    reshape x2 -> x0, local copies, waits for them, and re-layouts: 7.48 us -> none  [the longest x1 6.43 us: scan_forward(): return result.reshape(length_all, head_count * head_width)]
  transfers between devices with their start and end apart: 3 -> 0, of which waited for: 3 -> 0; matrix products, arithmetic and copies ran while one was open for 7% -> 0% of each run, Pallas kernels for 0% -> 0%
where the time goes in v1:
time: 76.5 us; the launch traced here: 75.9 us
  Pallas kernels  63.4 us (83%)
  local copies, waits for them, and re-layouts  11.2 us (15%)
  between operations  1.31 us (2%)
    pallas_call x1, Pallas kernels, compress(): pl.pallas_call(compress_kernel, out_shape=(jax.ShapeDtypeStruct((TOK, 2 *...  51 us
    pallas_call x1, Pallas kernels, scan_backward(): pl.pallas_call(scan_kernel, out_shape=(jax.ShapeDtypeStruct((TOK, COLS),...  12.4 us
    unnamed x15, local copies, waits for them, and re-layouts  11.2 us

profile of v1, /device:TPU:2, one launch (start us, length us, event | category | flops | bytes accessed | tf_op | source)
XLA Modules:
  0.0 75.9 jit_solution(12450809668586515028)
XLA Ops:
  1.3 1.1 %copy.13.ld_ref = f32[768,20]{1,0:T(8,128)S(1)} copy(f32[768,20]{0,1:T(8,128)} %param.13) | data formatting | bytes 122880 | tf_op args[4]
  2.3 0.0 copy-start
  2.3 1.5 %copy-done = bf16[768,1280]{1,0:T(8,128)(2,1)S(1)} copy-done((bf16[768,1280]{1,0:T(8,128)(2,1)S(1)}, bf16[768,1280]{1,0:T(8,128)(2,1)}, u32[]{:S(2)}) %copy-start) | copy-done | bytes 1966104
  3.9 0.0 copy-start.2
  3.9 0.9 %copy-done.2 = bf16[768,128]{1,0:T(8,128)(2,1)S(1)} copy-done((bf16[768,128]{1,0:T(8,128)(2,1)S(1)}, bf16[768,128]{1,0:T(8,128)(2,1)}, u32[]{:S(2)}) %copy-start.2) | copy-done | bytes 196632
  4.8 0.0 copy-start.3
  4.8 0.9 %copy-done.3 = bf16[768,128]{1,0:T(8,128)(2,1)S(1)} copy-done((bf16[768,128]{1,0:T(8,128)(2,1)S(1)}, bf16[768,128]{1,0:T(8,128)(2,1)}, u32[]{:S(2)}) %copy-start.3) | copy-done | bytes 196632
  5.7 0.0 copy-start.4
  5.7 0.7 copy-done.4
  6.4 0.0 copy-start.1
  6.4 12.4 %shard_map.120 = (bf16[768,1280]{1,0:T(8,128)(2,1)S(1)}, f32[768,256]{1,0:T(8,128)S(1)}) custom-call(bf16[768,1280]{1,0:T(8,128)(2,1)S(1)} %copy-done, bf16[768,1280]{1,0:T(8,128)(2,1)} %dy_ref.1, bf16[768,128]{1,0:T(8,128)(2,1)S(1)} %copy-done.2, bf16[768,128]{1,0:T(8,128)(2,1)S(1)} %copy-done.3, f32[768,20]{1,0:T(8,128)S(1)} %copy.13.ld_ref, ...), custom_call_target="tpu_custom_call" | custom-call | flops 2013265920 | bytes 8000000 | tf_op jit(solution)/shard_map/pallas_call | solution.py:152
  18.8 0.0 copy-done.1
  18.8 51.0 %shard_map.121 = (f32[768,256]{1,0:T(8,128)S(1)}, f32[32,1280]{1,0:T(8,128)S(1)}, f32[32,1280]{1,0:T(8,128)S(1)}, bf16[1,1280,1280]{2,1,0:T(8,128)(2,1)}) custom-call(s32[1]{0:T(128)S(6)} %copy.18.seed_ref, bf16[768,1280]{1,0:T(8,128)(2,1)S(1)} %copy-done.1, bf16[768,1280]{1,0:T(8,128)(2,1)S(1)} %get-tuple-element.6.gx_ref, bf16[1280,1280]{1,0:T(8,128)(2,1)} %bitcast.3, ...), custom_call_target="tpu_custom_call" | custom-call | flops 3604480000 | bytes 14000000 | tf_op jit(solution)/shard_map/pallas_call | solution.py:407
  69.9 0.9 %copy.19 = f32[768,256]{1,0:T(8,128)} copy(f32[768,256]{1,0:T(8,128)S(1)} %get-tuple-element.12) | data formatting | bytes 1572864
  70.7 0.7 copy.20
  71.4 0.7 copy.21
  72.1 3.8 %copy.22 = bf16[1,1280,1280]{2,1,0:T(8,128)(2,1)} copy(bf16[1,1280,1280]{2,1,0:T(8,128)(2,1)} %get-tuple-element.15) | data formatting | bytes 6553600
Async XLA Ops:
  2.3 1.6 %copy-start = (bf16[768,1280]{1,0:T(8,128)(2,1)S(1)}, bf16[768,1280]{1,0:T(8,128)(2,1)}, u32[]{:S(2)}) copy-start(bf16[768,1280]{1,0:T(8,128)(2,1)} %x_ref.1) | copy-start | bytes 5898244
  3.9 0.9 %copy-start.2 = (bf16[768,128]{1,0:T(8,128)(2,1)S(1)}, bf16[768,128]{1,0:T(8,128)(2,1)}, u32[]{:S(2)}) copy-start(bf16[768,128]{1,0:T(8,128)(2,1)} %b_ref.1) | copy-start | bytes 589828
  4.8 0.9 %copy-start.3 = (bf16[768,128]{1,0:T(8,128)(2,1)S(1)}, bf16[768,128]{1,0:T(8,128)(2,1)}, u32[]{:S(2)}) copy-start(bf16[768,128]{1,0:T(8,128)(2,1)} %c_ref.1) | copy-start | bytes 589828
  5.7 0.7 copy-start.4
  6.4 12.4 %copy-start.1 = (bf16[768,1280]{1,0:T(8,128)(2,1)S(1)}, bf16[768,1280]{1,0:T(8,128)(2,1)}, u32[]{:S(2)}) copy-start(bf16[768,1280]{1,0:T(8,128)(2,1)} %feat_ref.1) | copy-start | bytes 5898244

commit v2 on v1

v2 whole, which is shorter than its diff:
```python
import jax
import jax.numpy as jnp
from jax import lax
from jax.experimental import pallas as pl
from jax.experimental.pallas import tpu as pltpu
from jax.sharding import PartitionSpec as P

R = 32
TOK = 768
D = 1280
COLS = 1280
HEADS = 20
N = 128
BLK = 128
NB = TOK // BLK
PAIRS = HEADS // 2
NX, NY, NZ = 4, 4, 8
PLANE = NX * NY
PR, PC = 8, 384
WIDE = NY * PC
ROWS = 256
F32 = jnp.float32
BF16 = jnp.bfloat16
MESH = pl.DeviceIdType.MESH
VMEM = pltpu.VMEM
MIB = 1024 * 1024

NN = (((1,), (0,)), ((), ()))
NT = (((1,), (1,)), ((), ()))
TN = (((0,), (0,)), ((), ()))


def hops(k, size):
    return min(k, size - k)


IN_PLANE = sorted(range(1, PLANE), key=lambda k: -hops(k // NX, NY) - hops(k % NX, NX))
ON_LINE = sorted(range(1, NZ), key=lambda k: -hops(k, NZ))


def mm(a, b, dims=NN):
    return lax.dot_general(a, b, dims, preferred_element_type=F32)


def exact(a, b):
    return lax.dot_general(a, b, NN, precision=lax.Precision.HIGHEST, preferred_element_type=F32)


def split2(v):
    hi = v.astype(BF16)
    lo = (v - hi.astype(F32)).astype(BF16)
    return hi, lo


def split3(v):
    hi = v.astype(BF16)
    rest = v - hi.astype(F32)
    mid = rest.astype(BF16)
    lo = (rest - mid.astype(F32)).astype(BF16)
    return hi, mid, lo


def stack3(v):
    return jnp.concatenate(split3(v), axis=0)


def fold3(v):
    return v[0:R] + v[R : 2 * R] + v[2 * R : 3 * R]


def iota(shape, dim):
    return lax.broadcasted_iota(jnp.int32, shape, dim)


def block(c):
    return pl.ds(pl.multiple_of(c * BLK, BLK), BLK)


def mod(a):
    quotient = (a.astype(F32) * (1.0 / 46337.0)).astype(jnp.int32)
    left = a - quotient * 46337
    left = jnp.where(left < 0, left + 46337, left)
    return jnp.where(left >= 46337, left - 46337, left)


def start_factor(seed, offset):
    rank = iota((R, COLS), 0)
    column = iota((R, COLS), 1) + offset
    one = mod(rank * 7919 + column * 104 + seed)
    two = mod(one * one)
    three = mod(two * 211 + column * 13 + rank)
    four = mod(three * three)
    return four.astype(F32) * (2.0 / 46337.0) - 1.0


def inverse_factor(gram):
    work = jnp.concatenate(
        [gram, (iota((R, R), 0) == iota((R, R), 1)).astype(F32), jnp.zeros((R, 128 - 2 * R), F32)], axis=1
    )
    row_at = iota((R, 128), 0)
    diag = jnp.ones((R, 128), F32)
    for k in range(R):
        column = jnp.broadcast_to(work[:, k : k + 1], (R, 128))
        pivot = column[k : k + 1, :]
        diag = jnp.where(row_at == k, pivot, diag)
        scaled = work[k : k + 1, :] / pivot
        work = work - jnp.where(row_at > k, column, 0.0) * scaled
    return (work * lax.rsqrt(diag))[:, R : 2 * R]


class Comm:
    def __init__(self, local, full, slots, line, sems):
        self.local, self.full, self.slots, self.line, self.sems = local, full, slots, line, sems
        at = lax.axis_index("dp")
        self.core = lax.axis_index("tensor")
        self.x = lax.rem(at, NX)
        self.z = lax.rem(at // NX, NZ)
        self.y = at // (NX * NZ)

    def device(self, y, z, x):
        return ((y * NZ + z) * NX + x, self.core)

    def neighbour(self, k):
        return lax.rem(self.y + k // NX, NY), lax.rem(self.x + k % NX, NX)

    def greet(self, barrier):
        for k in IN_PLANE:
            y, x = self.neighbour(k)
            pl.semaphore_signal(barrier, inc=1, device_id=self.device(y, self.z, x), device_id_type=MESH)
        for k in ON_LINE:
            z = lax.rem(self.z + k, NZ)
            pl.semaphore_signal(barrier, inc=1, device_id=self.device(self.y, z, self.x), device_id_type=MESH)

    def piece(self, ref, y, x):
        return ref.at[pl.ds(pl.multiple_of(x * PR, PR), PR), pl.ds(pl.multiple_of(y * PC, 128), PC)]

    def scatter(self, k):
        y, x = self.neighbour(k)
        return pltpu.make_async_remote_copy(
            src_ref=self.piece(self.local, y, x),
            dst_ref=self.slots.at[k],
            send_sem=self.sems.at[0, k],
            recv_sem=self.sems.at[1, k],
            device_id=self.device(y, self.z, x),
            device_id_type=MESH,
        )

    def along(self, k):
        return pltpu.make_async_remote_copy(
            src_ref=self.line.at[self.z],
            dst_ref=self.line.at[self.z],
            send_sem=self.sems.at[2, k],
            recv_sem=self.sems.at[3, k],
            device_id=self.device(self.y, lax.rem(self.z + k, NZ), self.x),
            device_id_type=MESH,
        )

    def gather(self, k):
        y, x = self.neighbour(k)
        mine = self.piece(self.full, self.y, self.x)
        return pltpu.make_async_remote_copy(
            src_ref=mine,
            dst_ref=mine,
            send_sem=self.sems.at[4, k],
            recv_sem=self.sems.at[5, k],
            device_id=self.device(y, self.z, x),
            device_id_type=MESH,
        )

    def begin(self):
        for k in IN_PLANE:
            self.scatter(k).start()

    def middle(self):
        total = self.piece(self.local, self.y, self.x)[...]
        for k in IN_PLANE[::-1]:
            self.scatter(k).wait_recv()
            total = total + self.slots[k]
        self.line[self.z] = total
        for k in ON_LINE:
            self.along(k).start()

    def last(self):
        for k in ON_LINE[::-1]:
            self.along(k).wait_recv()
        total = self.line[0]
        for k in range(1, NZ):
            total = total + self.line[k]
        self.piece(self.full, self.y, self.x)[...] = total
        for k in IN_PLANE:
            self.gather(k).start()

    def end(self):
        for k in IN_PLANE[::-1]:
            self.gather(k).wait_recv()

    def settle(self):
        for k in IN_PLANE:
            self.scatter(k).wait_send()
            self.gather(k).wait_send()
        for k in ON_LINE:
            self.along(k).wait_send()


def main_kernel(
    seed_ref, feat_hbm, x_hbm, b_hbm, c_hbm, ld_hbm, gain_hbm, dy_hbm, err_hbm,
    whole_hbm, p_out, q_out, gbc_out, left_out, right_out,
    whole, feat, xin, dy, err, b_in, c_in, ld_in, gain_in, gx,
    ldp, gainp, gain_row, remain, decays, dys, after, after16, state, passing,
    start, through, first_part, gbc, other,
    local_p, full_p, slots_p, line_p, local_q, full_q, slots_q, line_q,
    sems_p, sems_q, pair_sems, in_sems, dy_sems, err_sems, whole_sems,
):
    first = Comm(local_p, full_p, slots_p, line_p, sems_p)
    second = Comm(local_q, full_q, slots_q, line_q, sems_q)
    core = first.core
    at = lax.axis_index("dp")

    def dy_copy(c):
        return pltpu.make_async_copy(dy_hbm.at[block(c), :], dy.at[block(c), :], dy_sems.at[c])

    def err_copy(i):
        rows = pl.ds(pl.multiple_of(i * ROWS, ROWS), ROWS)
        return pltpu.make_async_copy(err_hbm.at[rows, :], err.at[rows, :], err_sems.at[i])

    small = [(ld_hbm, ld_in), (b_hbm, b_in), (c_hbm, c_in), (gain_hbm, gain_in)]
    small = [pltpu.make_async_copy(s, d, in_sems.at[i]) for i, (s, d) in enumerate(small)]
    feat_copy = pltpu.make_async_copy(feat_hbm, feat, in_sems.at[4])
    x_copy = pltpu.make_async_copy(x_hbm, xin, in_sems.at[5])
    for copy in small:
        copy.start()
    for c in range(NB - 1, -1, -1):
        dy_copy(c).start()
    for i in range(D // ROWS):
        err_copy(i).start()
    feat_copy.start()
    x_copy.start()

    barrier = pltpu.get_barrier_semaphore()
    first.greet(barrier)
    pl.semaphore_signal(barrier, inc=1, device_id=(at, 1 - core), device_id_type=MESH)

    local_p[:, D:] = jnp.zeros((R, WIDE - D), F32)
    local_q[:, D:] = jnp.zeros((R, WIDE - D), F32)
    ldp[...] = jnp.zeros((128, TOK), F32)
    gainp[...] = jnp.zeros((8, 128), F32)
    after[...] = jnp.zeros((N, COLS), F32)
    state[...] = jnp.zeros((N, COLS), F32)
    start[...] = stack3(start_factor(seed_ref[0], core * COLS))
    expand = (iota((128, COLS), 0) == iota((128, COLS), 1) // 64).astype(BF16)
    expand2 = jnp.concatenate([expand, expand], axis=0)
    lower = (iota((BLK, BLK), 0) >= iota((BLK, BLK), 1)).astype(BF16)
    lower3 = jnp.concatenate([lower, lower, lower], axis=1)
    causal = iota((BLK, BLK), 0) <= iota((BLK, BLK), 1)
    causal2 = jnp.concatenate([causal, causal], axis=1)
    low_half = iota((BLK, 128), 1) < 64

    for copy in small:
        copy.wait()
    ldp[0:HEADS, :] = ld_in[...]
    gainp[0:1, 0:HEADS] = gain_in[...]
    gain_hi, gain_mid, gain_lo = split3(gainp[...])
    gain_row[...] = mm(gain_hi, expand) + mm(gain_mid, expand) + mm(gain_lo, expand)

    def masked(dy_pair):
        zero = jnp.zeros_like(dy_pair)
        return jnp.concatenate([jnp.where(low_half, dy_pair, zero), jnp.where(low_half, zero, dy_pair)], axis=0)

    def token_block(c, more):
        rows = block(c)
        dy_copy(c).wait()
        turned = mm(jnp.concatenate(split3(ldp[:, rows]), axis=1), lower3, NT)
        total = turned.T
        factors = jnp.concatenate([jnp.exp(total), jnp.exp(total[BLK - 1 : BLK, :] - total)], axis=0)
        wide = mm(jnp.concatenate(split2(factors), axis=1), expand2)
        grow, left = wide[:BLK], wide[BLK:]
        remain[rows, :] = left
        passing[pl.ds(pl.multiple_of(8 * c, 8), 8), :] = grow[BLK - 8 : BLK]
        dy_scaled, dy_rest = split2(dy[rows, :].astype(F32) * grow)
        dys[rows, :] = dy_scaled
        b_blk, c_blk = b_in[rows, :], c_in[rows, :]
        now = after[...]
        now16, now_rest = split2(now)
        after16[rows, :] = now16
        carried = mm(jnp.concatenate([b_blk, b_blk], axis=1), jnp.concatenate([now16, now_rest], axis=0)) * left
        scores = mm(b_blk, c_blk, NT)
        scores2 = jnp.concatenate([scores, scores], axis=1)
        for j in range(PAIRS):
            lanes = slice(128 * j, 128 * j + 128)
            dy_pair = dy[rows, lanes]
            both = masked(dy_pair)
            h = 2 * j
            to_row = jnp.concatenate([turned[h : h + 1, :], turned[h + 1 : h + 2, :]], axis=1)
            from_col = jnp.concatenate(
                [
                    jnp.broadcast_to(total[:, h : h + 1], (BLK, BLK)),
                    jnp.broadcast_to(total[:, h + 1 : h + 2], (BLK, BLK)),
                ],
                axis=1,
            )
            decay = jnp.exp(jnp.where(causal2, to_row - from_col, -1e30))
            decays[rows, 256 * j : 256 * j + 256] = decay
            weights, weights_rest = split2(decay * scores2)
            grad_x = mm(weights, both) + mm(weights_rest, both)
            grad_x = grad_x + gain_row[0:1, lanes] * dy_pair.astype(F32) + carried[:, lanes]
            gx[rows, lanes] = grad_x.astype(BF16)
        through[:, rows] = fold3(mm(start[...], gx[rows, :], NT))
        if more:
            after[...] = now * grow[BLK - 1 : BLK] + mm(
                jnp.concatenate([c_blk, c_blk], axis=0), jnp.concatenate([dy_scaled, dy_rest], axis=0), TN
            )
            i = NB - 1 - c
            rows = pl.ds(pl.multiple_of(i * ROWS, ROWS), ROWS)
            err_copy(i).wait()
            first_part[:, rows] = fold3(mm(start[...], err[rows, :], NT))

    def step(i, carry):
        token_block(NB - 1 - i, True)
        return carry

    lax.fori_loop(0, NB - 1, step, 0)
    token_block(0, False)
    feat_copy.wait()
    local_p[:, :D] = first_part[...] + fold3(mm(stack3(through[...]), feat[...])) * (1.0 / TOK)

    pl.semaphore_wait(barrier, PLANE - 1 + NZ - 1 + 1)
    first.begin()

    def whole_rows(i):
        rows = pl.ds(i * ROWS, ROWS)
        part = mm(feat[:, i * ROWS : (i + 1) * ROWS], gx[...], TN)
        whole[rows, :] = part * (1.0 / TOK) + err[rows, :].astype(F32)
        copy = pltpu.make_async_copy(whole.at[rows, :], whole_hbm.at[rows, :], whole_sems.at[i])
        copy.start()
        return copy

    def bc_block(c, carry):
        rows = block(c)
        b_blk, c_blk = b_in[rows, :], c_in[rows, :]
        x_scaled = (xin[rows, :].astype(F32) * remain[rows, :]).astype(BF16)
        before = state[...]
        grad_b = mm(x_scaled, after16[rows, :], NT)
        grad_c = mm(dys[rows, :], before.astype(BF16), NT)
        factor = passing[pl.ds(pl.multiple_of(8 * c, 8), 8), :][7:8, :]
        state[...] = before * factor + mm(b_blk, x_scaled, TN)
        gaps = jnp.zeros((BLK, BLK), F32)
        for j in range(PAIRS):
            lanes = slice(128 * j, 128 * j + 128)
            products = mm(xin[rows, lanes], masked(dy[rows, lanes]), NT) * decays[rows, 256 * j : 256 * j + 256]
            gaps = gaps + products[:, :BLK] + products[:, BLK:]
        gap_hi, gap_lo = split2(gaps)
        gbc[rows, 0:N] = grad_b + mm(gap_hi, c_blk) + mm(gap_lo, c_blk)
        gbc[rows, N : 2 * N] = grad_c + mm(gap_hi, b_blk, TN) + mm(gap_lo, b_blk, TN)
        return carry

    whole_copies = [whole_rows(i) for i in range(D // ROWS)]
    first.middle()
    x_copy.wait()
    lax.fori_loop(0, NB // 2, bc_block, 0)
    first.last()
    lax.fori_loop(NB // 2, NB, bc_block, 0)
    swap = pltpu.make_async_remote_copy(
        src_ref=gbc,
        dst_ref=other,
        send_sem=pair_sems.at[0],
        recv_sem=pair_sems.at[1],
        device_id=(at, 1 - core),
        device_id_type=MESH,
    )
    swap.start()
    first.end()

    psum = full_p[:, :D]
    parts = stack3(psum)
    inner = fold3(mm(parts, feat[...], NT))
    local_q[:, :COLS] = fold3(mm(parts, err[...]) + mm(stack3(inner), gx[...]) * (1.0 / TOK))
    second.begin()

    cross = mm(parts, parts, NT)
    gram = jnp.zeros((R, R), F32)
    for a in range(2, -1, -1):
        for b in range(2, -1, -1):
            gram = gram + cross[R * a : R * a + R, R * b : R * b + R]
    inverse = inverse_factor(gram)
    second.middle()

    basis = exact(inverse, psum)
    p_out[...] = basis
    p_hi, p_lo = split2(basis * (1.0 / 128.0))
    left_out[...] = jnp.concatenate([p_hi, p_hi, p_lo, p_lo], axis=0).T
    second.last()

    swap.wait()
    gbc_out[...] = gbc[...] + other[...]
    first.settle()
    second.end()

    summed = exact(inverse, full_q[:, :COLS])
    q_out[...] = summed
    q_hi, q_lo = split2(summed)
    right_out[...] = jnp.concatenate([q_hi, q_lo, q_hi, q_lo], axis=0)
    second.settle()
    for copy in whole_copies:
        copy.wait()


def last_kernel(
    whole_hbm, p_in, q_in, gbc_in, left_hbm, right_hbm, gbc_out, p_out, q_out, err_out,
    whole, left, right, done, p, q, gbc, sems, in_sems, out_sems,
):
    def part(i):
        return pl.ds(i * ROWS, ROWS)

    factors = [
        pltpu.make_async_copy(left_hbm, left, sems.at[0]),
        pltpu.make_async_copy(right_hbm, right, sems.at[1]),
    ]
    loads = [
        pltpu.make_async_copy(whole_hbm.at[part(i), :], whole.at[part(i), :], in_sems.at[i]) for i in range(D // ROWS)
    ]
    passed = [(p_in, p, p_out), (q_in, q, q_out), (gbc_in, gbc, gbc_out)]
    arriving = [pltpu.make_async_copy(v[0], v[1], sems.at[2 + i]) for i, v in enumerate(passed)]
    copies = [pltpu.make_async_copy(v[1], v[2], sems.at[5 + i]) for i, v in enumerate(passed)]
    for copy in factors + loads + arriving:
        copy.start()
    for copy in factors:
        copy.wait()
    for i in range(D // ROWS):
        change = mm(left[part(i), :], right[...])
        loads[i].wait()
        done[part(i), :] = (whole[part(i), :] - change).astype(BF16)
        copy = pltpu.make_async_copy(done.at[part(i), :], err_out.at[0, part(i), :], out_sems.at[i])
        copy.start()
        copies.append(copy)
        if i == 1:
            for into, out in zip(arriving, copies):
                into.wait()
                out.start()
    for copy in copies:
        copy.wait()


def body(layer_in, ssm_in, b_in, c_in, log_decay, skip_gain, grad_out, q_seed, error_in):
    vm = pl.BlockSpec(memory_space=VMEM)
    hbm = pl.BlockSpec(memory_space=pltpu.HBM)
    piece = VMEM((R, WIDE), F32)
    slots = VMEM((PLANE, PR, PC), F32)
    line = VMEM((NZ, PR, PC), F32)
    tokens16 = VMEM((TOK, COLS), BF16)
    tokens32 = VMEM((TOK, COLS), F32)
    dma = pltpu.SemaphoreType.DMA
    whole, p, q, gbc, left, right = pl.pallas_call(
        main_kernel,
        out_shape=(
            jax.ShapeDtypeStruct((D, COLS), F32),
            jax.ShapeDtypeStruct((R, D), F32),
            jax.ShapeDtypeStruct((R, COLS), F32),
            jax.ShapeDtypeStruct((TOK, 2 * N), F32),
            jax.ShapeDtypeStruct((D, 4 * R), BF16),
            jax.ShapeDtypeStruct((4 * R, COLS), BF16),
        ),
        in_specs=[pl.BlockSpec(memory_space=pltpu.SMEM)] + [hbm] * 8,
        out_specs=[hbm] + [vm] * 5,
        scratch_shapes=[
            VMEM((D, COLS), F32),
            tokens16, tokens16, tokens16,
            VMEM((D, COLS), BF16),
            VMEM((TOK, N), BF16), VMEM((TOK, N), BF16),
            VMEM((HEADS, TOK), F32), VMEM((1, HEADS), F32),
            tokens16,
            VMEM((128, TOK), F32),
            VMEM((8, 128), F32), VMEM((8, COLS), F32),
            tokens32,
            VMEM((TOK, HEADS * BLK), F32),
            tokens16,
            VMEM((N, COLS), F32),
            tokens16,
            VMEM((N, COLS), F32),
            VMEM((8 * NB, COLS), F32),
            VMEM((3 * R, COLS), BF16),
            VMEM((R, TOK), F32),
            VMEM((R, D), F32),
            VMEM((TOK, 2 * N), F32), VMEM((TOK, 2 * N), F32),
            piece, piece, slots, line,
            piece, piece, slots, line,
            dma((6, PLANE)), dma((6, PLANE)), dma((2,)), dma((6,)), dma((NB,)), dma((D // ROWS,)), dma((D // ROWS,)),
        ],
        compiler_params=pltpu.CompilerParams(
            collective_id=0, has_side_effects=True, vmem_limit_bytes=62 * MIB
        ),
        cost_estimate=pl.CostEstimate(
            flops=2 * D * COLS * 2200, bytes_accessed=20_000_000, transcendentals=TOK * BLK * HEADS
        ),
    )(
        q_seed, layer_in, ssm_in, b_in, c_in, log_decay.T, skip_gain.reshape(1, HEADS), grad_out,
        error_in.reshape(D, COLS),
    )
    return pl.pallas_call(
        last_kernel,
        out_shape=(
            jax.ShapeDtypeStruct((TOK, 2 * N), F32),
            jax.ShapeDtypeStruct((R, D), F32),
            jax.ShapeDtypeStruct((R, COLS), F32),
            jax.ShapeDtypeStruct((1, D, COLS), BF16),
        ),
        in_specs=[hbm] * 6,
        out_specs=[hbm] * 4,
        scratch_shapes=[
            VMEM((D, COLS), F32), VMEM((D, 4 * R), BF16), VMEM((4 * R, COLS), BF16), VMEM((D, COLS), BF16),
            VMEM((R, D), F32), VMEM((R, COLS), F32), VMEM((TOK, 2 * N), F32), dma((8,)), dma((D // ROWS,)), dma((D // ROWS,)),
        ],
        compiler_params=pltpu.CompilerParams(vmem_limit_bytes=62 * MIB),
        cost_estimate=pl.CostEstimate(flops=2 * D * COLS * 128, bytes_accessed=11_000_000, transcendentals=0),
    )(whole, p, q, gbc, left, right)


def solution(mesh):
    in_specs = (
        P("dp", None),
        P("dp", "tensor"),
        P("dp", None),
        P("dp", None),
        P("dp", "tensor"),
        P("tensor"),
        P("dp", "tensor"),
        P(),
        P("dp", None, "tensor"),
    )
    out_specs = (P("dp", None), P("tensor", None), P(None, "tensor"), P("dp", None, "tensor"))
    return jax.shard_map(body, mesh=mesh, in_specs=in_specs, out_specs=out_specs, check_vma=False)
```

time: 76.5 us -> 64.2 us (0.84)
  local copies, waits for them, and re-layouts: 11.2 us -> 0 us
    unnamed x15 -> x0, local copies, waits for them, and re-layouts: 11.2 us -> none
where the time goes in v2:
time: 64.2 us; the launch traced here: 64.1 us
  Pallas kernels  62.8 us (98%)
  between operations  1.29 us (2%)
    pallas_call x1, Pallas kernels, body(): pl.pallas_call(main_kernel, out_shape=(jax.ShapeDtypeStruct((D, COLS), F3...  56.5 us
    pallas_call x1, Pallas kernels, body(): pl.pallas_call(last_kernel, out_shape=(jax.ShapeDtypeStruct((TOK, 2 * N),...  6.36 us

profile of v2, /device:TPU:2, one launch (start us, length us, event | category | flops | bytes accessed | tf_op | source)
XLA Modules:
  0.0 64.1 jit_solution(6034123419189960236)
XLA Ops:
  1.3 56.5 %shard_map.120 = (f32[1280,1280]{1,0:T(8,128)}, f32[32,1280]{1,0:T(8,128)}, f32[32,1280]{1,0:T(8,128)}, f32[768,256]{1,0:T(8,128)}, bf16[1280,128]{1,0:T(8,128)(2,1)}, /*index=5*/bf16[128,1280]{1,0:T(8,128)(2,1)}) custom-call(s32[1]{0:T(128)S(6)} %copy.13.seed_ref, bf16[768,1280]{1,0:T(8,128)(2,1)} %feat_hbm.1, bf16[768,1280]{1,0:T(8,128)(2,1)} %x_hbm.1, ...), custom_call_target="tpu_custom_call" | custom-call | flops 7208960000 | bytes 20000000 | tf_op jit(solution)/shard_map/pallas_call | solution.py:452
  57.7 6.4 %shard_map.121 = (f32[768,256]{1,0:T(8,128)}, f32[32,1280]{1,0:T(8,128)}, f32[32,1280]{1,0:T(8,128)}, bf16[1,1280,1280]{2,1,0:T(8,128)(2,1)}) custom-call(f32[1280,1280]{1,0:T(8,128)} %get-tuple-element.10.whole_hbm, f32[32,1280]{1,0:T(8,128)} %get-tuple-element.11.p_in, f32[32,1280]{1,0:T(8,128)} %get-tuple-element.12.q_in, ...), custom_call_target="tpu_custom_call" | custom-call | flops 419430400 | bytes 11000000 | tf_op jit(solution)/shard_map/pallas_call | solution.py:498

commit v3 on v2

--- a/solution.py
+++ b/solution.py
@@ -204,12 +204,12 @@
 
 def main_kernel(
     seed_ref, feat_hbm, x_hbm, b_hbm, c_hbm, ld_hbm, gain_hbm, dy_hbm, err_hbm,
-    whole_hbm, p_out, q_out, gbc_out, left_out, right_out,
-    whole, feat, xin, dy, err, b_in, c_in, ld_in, gain_in, gx,
+    whole, p_out, q_out, gbc_out, left_out, right_out,
+    feat, xin, dy, err, b_in, c_in, ld_in, gain_in, gx,
     ldp, gainp, gain_row, remain, decays, dys, after, after16, state, passing,
-    start, through, first_part, gbc, other,
+    start, first_part, gbc, other,
     local_p, full_p, slots_p, line_p, local_q, full_q, slots_q, line_q,
-    sems_p, sems_q, pair_sems, in_sems, dy_sems, err_sems, whole_sems,
+    sems_p, sems_q, pair_sems, in_sems, dy_sems, err_sems,
 ):
     first = Comm(local_p, full_p, slots_p, line_p, sems_p)
     second = Comm(local_q, full_q, slots_q, line_q, sems_q)
@@ -229,12 +229,7 @@
     x_copy = pltpu.make_async_copy(x_hbm, xin, in_sems.at[5])
     for copy in small:
         copy.start()
-    for c in range(NB - 1, -1, -1):
-        dy_copy(c).start()
-    for i in range(D // ROWS):
-        err_copy(i).start()
-    feat_copy.start()
-    x_copy.start()
+    dy_copy(NB - 1).start()
 
     barrier = pltpu.get_barrier_semaphore()
     first.greet(barrier)
@@ -246,7 +241,8 @@
     gainp[...] = jnp.zeros((8, 128), F32)
     after[...] = jnp.zeros((N, COLS), F32)
     state[...] = jnp.zeros((N, COLS), F32)
-    start[...] = stack3(start_factor(seed_ref[0], core * COLS))
+    factor3 = stack3(start_factor(seed_ref[0], core * COLS))
+    start[...] = jnp.concatenate([factor3, jnp.zeros((R, COLS), BF16)], axis=0).T
     expand = (iota((128, COLS), 0) == iota((128, COLS), 1) // 64).astype(BF16)
     expand2 = jnp.concatenate([expand, expand], axis=0)
     lower = (iota((BLK, BLK), 0) >= iota((BLK, BLK), 1)).astype(BF16)
@@ -257,6 +253,12 @@
 
     for copy in small:
         copy.wait()
+    for c in range(NB - 2, -1, -1):
+        dy_copy(c).start()
+    for i in range(D // ROWS):
+        err_copy(i).start()
+    feat_copy.start()
+    x_copy.start()
     ldp[0:HEADS, :] = ld_in[...]
     gainp[0:1, 0:HEADS] = gain_in[...]
     gain_hi, gain_mid, gain_lo = split3(gainp[...])
@@ -268,7 +270,6 @@
 
     def token_block(c, more):
         rows = block(c)
-        dy_copy(c).wait()
         turned = mm(jnp.concatenate(split3(ldp[:, rows]), axis=1), lower3, NT)
         total = turned.T
         factors = jnp.concatenate([jnp.exp(total), jnp.exp(total[BLK - 1 : BLK, :] - total)], axis=0)
@@ -304,24 +305,32 @@
             grad_x = mm(weights, both) + mm(weights_rest, both)
             grad_x = grad_x + gain_row[0:1, lanes] * dy_pair.astype(F32) + carried[:, lanes]
             gx[rows, lanes] = grad_x.astype(BF16)
-        through[:, rows] = fold3(mm(start[...], gx[rows, :], NT))
         if more:
             after[...] = now * grow[BLK - 1 : BLK] + mm(
                 jnp.concatenate([c_blk, c_blk], axis=0), jnp.concatenate([dy_scaled, dy_rest], axis=0), TN
             )
-            i = NB - 1 - c
-            rows = pl.ds(pl.multiple_of(i * ROWS, ROWS), ROWS)
-            err_copy(i).wait()
-            first_part[:, rows] = fold3(mm(start[...], err[rows, :], NT))
-
-    def step(i, carry):
-        token_block(NB - 1 - i, True)
-        return carry
-
-    lax.fori_loop(0, NB - 1, step, 0)
-    token_block(0, False)
-    feat_copy.wait()
-    local_p[:, :D] = first_part[...] + fold3(mm(stack3(through[...]), feat[...])) * (1.0 / TOK)
+
+    def project(low, high):
+        rows = slice(low * BLK, high * BLK)
+        return fold3(mm(stack3(fold3(mm(gx[rows, :], start[...]).T)), feat[rows, :]))
+
+    for c in range(NB - 1, -1, -1):
+        if c >= NB - 2:
+            dy_copy(c).wait()
+        elif c == NB - 3:
+            for k in range(NB - 3, -1, -1):
+                dy_copy(k).wait()
+            for i in range(D // ROWS):
+                err_copy(i).wait()
+        elif c == 0:
+            feat_copy.wait()
+            early = project(1, NB)
+        token_block(c, c > 0)
+        if NB - 3 >= c > 0:
+            for i in range(2 * (NB - 3 - c), min(2 * (NB - 3 - c) + 2, D // ROWS)):
+                rows = pl.ds(i * ROWS, ROWS)
+                first_part[:, rows] = fold3(mm(err[rows, :], start[...]).T)
+    local_p[:, :D] = first_part[...] + (early + project(0, 1)) * (1.0 / TOK)
 
     pl.semaphore_wait(barrier, PLANE - 1 + NZ - 1 + 1)
     first.begin()
@@ -330,9 +339,6 @@
         rows = pl.ds(i * ROWS, ROWS)
         part = mm(feat[:, i * ROWS : (i + 1) * ROWS], gx[...], TN)
         whole[rows, :] = part * (1.0 / TOK) + err[rows, :].astype(F32)
-        copy = pltpu.make_async_copy(whole.at[rows, :], whole_hbm.at[rows, :], whole_sems.at[i])
-        copy.start()
-        return copy
 
     def bc_block(c, carry):
         rows = block(c)
@@ -353,7 +359,8 @@
         gbc[rows, N : 2 * N] = grad_c + mm(gap_hi, b_blk, TN) + mm(gap_lo, b_blk, TN)
         return carry
 
-    whole_copies = [whole_rows(i) for i in range(D // ROWS)]
+    for i in range(D // ROWS):
+        whole_rows(i)
     first.middle()
     x_copy.wait()
     lax.fori_loop(0, NB // 2, bc_block, 0)
@@ -400,42 +407,22 @@
     q_hi, q_lo = split2(summed)
     right_out[...] = jnp.concatenate([q_hi, q_lo, q_hi, q_lo], axis=0)
     second.settle()
-    for copy in whole_copies:
-        copy.wait()
-
-
-def last_kernel(
-    whole_hbm, p_in, q_in, gbc_in, left_hbm, right_hbm, gbc_out, p_out, q_out, err_out,
-    whole, left, right, done, p, q, gbc, sems, in_sems, out_sems,
-):
-    def part(i):
-        return pl.ds(i * ROWS, ROWS)
-
-    factors = [
-        pltpu.make_async_copy(left_hbm, left, sems.at[0]),
-        pltpu.make_async_copy(right_hbm, right, sems.at[1]),
+
+
+def last_kernel(whole, p_in, q_in, gbc_in, left, right, gbc_out, p_out, q_out, err_out, done, sems, out_sems):
+    copies = [
+        pltpu.make_async_copy(gbc_in, gbc_out, sems.at[0]),
+        pltpu.make_async_copy(p_in, p_out, sems.at[1]),
+        pltpu.make_async_copy(q_in, q_out, sems.at[2]),
     ]
-    loads = [
-        pltpu.make_async_copy(whole_hbm.at[part(i), :], whole.at[part(i), :], in_sems.at[i]) for i in range(D // ROWS)
-    ]
-    passed = [(p_in, p, p_out), (q_in, q, q_out), (gbc_in, gbc, gbc_out)]
-    arriving = [pltpu.make_async_copy(v[0], v[1], sems.at[2 + i]) for i, v in enumerate(passed)]
-    copies = [pltpu.make_async_copy(v[1], v[2], sems.at[5 + i]) for i, v in enumerate(passed)]
-    for copy in factors + loads + arriving:
+    for copy in copies:
         copy.start()
-    for copy in factors:
-        copy.wait()
     for i in range(D // ROWS):
-        change = mm(left[part(i), :], right[...])
-        loads[i].wait()
-        done[part(i), :] = (whole[part(i), :] - change).astype(BF16)
-        copy = pltpu.make_async_copy(done.at[part(i), :], err_out.at[0, part(i), :], out_sems.at[i])
+        rows = pl.ds(i * ROWS, ROWS)
+        done[rows, :] = (whole[rows, :] - mm(left[rows, :], right[...])).astype(BF16)
+        copy = pltpu.make_async_copy(done.at[rows, :], err_out.at[0, rows, :], out_sems.at[i])
         copy.start()
         copies.append(copy)
-        if i == 1:
-            for into, out in zip(arriving, copies):
-                into.wait()
-                out.start()
     for copy in copies:
         copy.wait()
 
@@ -449,20 +436,19 @@
     tokens16 = VMEM((TOK, COLS), BF16)
     tokens32 = VMEM((TOK, COLS), F32)
     dma = pltpu.SemaphoreType.DMA
-    whole, p, q, gbc, left, right = pl.pallas_call(
+    held = pl.pallas_call(
         main_kernel,
         out_shape=(
-            jax.ShapeDtypeStruct((D, COLS), F32),
-            jax.ShapeDtypeStruct((R, D), F32),
-            jax.ShapeDtypeStruct((R, COLS), F32),
-            jax.ShapeDtypeStruct((TOK, 2 * N), F32),
-            jax.ShapeDtypeStruct((D, 4 * R), BF16),
-            jax.ShapeDtypeStruct((4 * R, COLS), BF16),
+            VMEM((D, COLS), F32),
+            VMEM((R, D), F32),
+            VMEM((R, COLS), F32),
+            VMEM((TOK, 2 * N), F32),
+            VMEM((D, 4 * R), BF16),
+            VMEM((4 * R, COLS), BF16),
         ),
         in_specs=[pl.BlockSpec(memory_space=pltpu.SMEM)] + [hbm] * 8,
-        out_specs=[hbm] + [vm] * 5,
+        out_specs=[vm] * 6,
         scratch_shapes=[
-            VMEM((D, COLS), F32),
             tokens16, tokens16, tokens16,
             VMEM((D, COLS), BF16),
             VMEM((TOK, N), BF16), VMEM((TOK, N), BF16),
@@ -477,23 +463,28 @@
             tokens16,
             VMEM((N, COLS), F32),
             VMEM((8 * NB, COLS), F32),
-            VMEM((3 * R, COLS), BF16),
-            VMEM((R, TOK), F32),
+            VMEM((COLS, 4 * R), BF16),
             VMEM((R, D), F32),
             VMEM((TOK, 2 * N), F32), VMEM((TOK, 2 * N), F32),
             piece, piece, slots, line,
             piece, piece, slots, line,
-            dma((6, PLANE)), dma((6, PLANE)), dma((2,)), dma((6,)), dma((NB,)), dma((D // ROWS,)), dma((D // ROWS,)),
+            dma((6, PLANE)), dma((6, PLANE)), dma((2,)), dma((6,)), dma((NB,)), dma((D // ROWS,)),
         ],
         compiler_params=pltpu.CompilerParams(
-            collective_id=0, has_side_effects=True, vmem_limit_bytes=62 * MIB
+            collective_id=0, has_side_effects=True, vmem_limit_bytes=44 * MIB
         ),
         cost_estimate=pl.CostEstimate(
             flops=2 * D * COLS * 2200, bytes_accessed=20_000_000, transcendentals=TOK * BLK * HEADS
         ),
     )(
-        q_seed, layer_in, ssm_in, b_in, c_in, log_decay.T, skip_gain.reshape(1, HEADS), grad_out,
-        error_in.reshape(D, COLS),
+        q_seed,
+        *(
+            pltpu.with_memory_space_constraint(v, pltpu.HBM)
+            for v in (
+                layer_in, ssm_in, b_in, c_in, log_decay.T, skip_gain.reshape(1, HEADS), grad_out,
+                error_in.reshape(D, COLS),
+            )
+        ),
     )
     return pl.pallas_call(
         last_kernel,
@@ -503,15 +494,12 @@
             jax.ShapeDtypeStruct((R, COLS), F32),
             jax.ShapeDtypeStruct((1, D, COLS), BF16),
         ),
-        in_specs=[hbm] * 6,
+        in_specs=[vm] * 6,
         out_specs=[hbm] * 4,
-        scratch_shapes=[
-            VMEM((D, COLS), F32), VMEM((D, 4 * R), BF16), VMEM((4 * R, COLS), BF16), VMEM((D, COLS), BF16),
-            VMEM((R, D), F32), VMEM((R, COLS), F32), VMEM((TOK, 2 * N), F32), dma((8,)), dma((D // ROWS,)), dma((D // ROWS,)),
-        ],
-        compiler_params=pltpu.CompilerParams(vmem_limit_bytes=62 * MIB),
+        scratch_shapes=[VMEM((D, COLS), BF16), dma((3,)), dma((D // ROWS,))],
+        compiler_params=pltpu.CompilerParams(vmem_limit_bytes=16 * MIB),
         cost_estimate=pl.CostEstimate(flops=2 * D * COLS * 128, bytes_accessed=11_000_000, transcendentals=0),
-    )(whole, p, q, gbc, left, right)
+    )(*(pltpu.with_memory_space_constraint(v, VMEM) for v in held))
 
 
 def solution(mesh):

time: 64.2 us -> 56.8 us (0.88)
  Pallas kernels: 62.8 us -> 55.2 us
    pallas_call x1, Pallas kernels: 6.36 us -> 2.2 us  [body(): pl.pallas_call(last_kernel, out_shape=(jax.ShapeDtypeStruct((TOK, 2 * N),...]
    pallas_call x1, Pallas kernels: 56.5 us -> 53 us  [body(): pl.pallas_call(main_kernel, out_shape=(VMEM((D, COLS), F32), VMEM((R, D),...]
where the time goes in v3:
time: 56.8 us; the launch traced here: 56.7 us
  Pallas kernels  55.2 us (97%)
  between operations  1.45 us (3%)
    pallas_call x1, Pallas kernels, body(): pl.pallas_call(main_kernel, out_shape=(VMEM((D, COLS), F32), VMEM((R, D),...  53 us
    pallas_call x1, Pallas kernels, body(): pl.pallas_call(last_kernel, out_shape=(jax.ShapeDtypeStruct((TOK, 2 * N),...  2.2 us

profile of v3, /device:TPU:2, one launch (start us, length us, event | category | flops | bytes accessed | tf_op | source)
XLA Modules:
  0.0 56.7 jit_solution(1668245782770479256)
XLA Ops:
  1.3 53.0 %shard_map.120 = (f32[1280,1280]{1,0:T(8,128)S(1)}, f32[32,1280]{1,0:T(8,128)S(1)}, f32[32,1280]{1,0:T(8,128)S(1)}, f32[768,256]{1,0:T(8,128)S(1)}, bf16[1280,12...) custom-call(s32[1]{0:T(128)S(6)} %copy.13.seed_ref, bf16[768,1280]{1,0:T(8,128)(2,1)} %feat_hbm.1, ...), custom_call_target="tpu_custom_call" | custom-call | flops 7208960000 | bytes 20000000 | tf_op jit(solution)/shard_map/pallas_call | solution.py:439
  54.3 2.2 %shard_map.121 = (f32[768,256]{1,0:T(8,128)}, f32[32,1280]{1,0:T(8,128)}, f32[32,1280]{1,0:T(8,128)}, bf16[1,1280,1280]{2,1,0:T(8,128)(2,1)}) custom-call(f32[1280,1280]{1,0:T(8,128)S(1)} %get-tuple-element.10.whole, f32[32,1280]{1,0:T(8,128)S(1)} %get-tuple-element.11.p_in, f32[32,1280]{1,0:T(8,128)S(1)} %get-tuple-element.12.q_in, ...), custom_call_target="tpu_custom_call" | custom-call | flops 419430400 | bytes 11000000 | tf_op jit(solution)/shard_map/pallas_call | solution.py:489

commit v4 on v3

--- a/solution.py
+++ b/solution.py
@@ -36,14 +36,21 @@
 
 IN_PLANE = sorted(range(1, PLANE), key=lambda k: -hops(k // NX, NY) - hops(k % NX, NX))
 ON_LINE = sorted(range(1, NZ), key=lambda k: -hops(k, NZ))
+NEAR_FIRST = sorted(range(NY), key=lambda k: hops(k, NY))
 
 
 def mm(a, b, dims=NN):
     return lax.dot_general(a, b, dims, preferred_element_type=F32)
 
 
-def exact(a, b):
-    return lax.dot_general(a, b, NN, precision=lax.Precision.HIGHEST, preferred_element_type=F32)
+def narrow(a, b):
+    a1, a2, a3 = split3(a)
+    b1, b2, b3 = split3(b)
+    zero = jnp.zeros((R, 2 * R), BF16)
+    return mm(
+        jnp.concatenate([a1, a1, a2, a1, a2, a3, zero], axis=1),
+        jnp.concatenate([b1, b2, b1, b3, b2, b1, b1, b1], axis=0),
+    )
 
 
 def split2(v):
@@ -190,9 +197,15 @@
         for k in IN_PLANE:
             self.gather(k).start()
 
+    def end_part(self, dy):
+        for k in range(NX * dy, NX * dy + NX):
+            if k:
+                self.gather(k).wait_recv()
+        return lax.rem(self.y + NY - dy, NY)
+
     def end(self):
-        for k in IN_PLANE[::-1]:
-            self.gather(k).wait_recv()
+        for dy in NEAR_FIRST:
+            self.end_part(dy)
 
     def settle(self):
         for k in IN_PLANE:
@@ -204,9 +217,9 @@
 
 def main_kernel(
     seed_ref, feat_hbm, x_hbm, b_hbm, c_hbm, ld_hbm, gain_hbm, dy_hbm, err_hbm,
-    whole, p_out, q_out, gbc_out, left_out, right_out,
+    whole_hi, whole_lo, p_out, q_out, gbc_out, left_out, right_out,
     feat, xin, dy, err, b_in, c_in, ld_in, gain_in, gx,
-    ldp, gainp, gain_row, remain, decays, dys, after, after16, state, passing,
+    ldp, gainp, gain_row, grows, remain, decays, dys, after, after16, state, passing,
     start, first_part, gbc, other,
     local_p, full_p, slots_p, line_p, local_q, full_q, slots_q, line_q,
     sems_p, sems_q, pair_sems, in_sems, dy_sems, err_sems,
@@ -237,6 +250,8 @@
 
     local_p[:, D:] = jnp.zeros((R, WIDE - D), F32)
     local_q[:, D:] = jnp.zeros((R, WIDE - D), F32)
+    whole_hi[D:, :] = jnp.zeros((WIDE - D, COLS), BF16)
+    whole_lo[D:, :] = jnp.zeros((WIDE - D, COLS), BF16)
     ldp[...] = jnp.zeros((128, TOK), F32)
     gainp[...] = jnp.zeros((8, 128), F32)
     after[...] = jnp.zeros((N, COLS), F32)
@@ -248,7 +263,6 @@
     lower = (iota((BLK, BLK), 0) >= iota((BLK, BLK), 1)).astype(BF16)
     lower3 = jnp.concatenate([lower, lower, lower], axis=1)
     causal = iota((BLK, BLK), 0) <= iota((BLK, BLK), 1)
-    causal2 = jnp.concatenate([causal, causal], axis=1)
     low_half = iota((BLK, 128), 1) < 64
 
     for copy in small:
@@ -264,19 +278,24 @@
     gain_hi, gain_mid, gain_lo = split3(gainp[...])
     gain_row[...] = mm(gain_hi, expand) + mm(gain_mid, expand) + mm(gain_lo, expand)
 
+    turns = [mm(jnp.concatenate(split3(ldp[:, block(c)]), axis=1), lower3, NT) for c in range(NB)]
+    totals = [turned.T for turned in turns]
+    begun = jnp.concatenate([jnp.exp(total) for total in totals], axis=0)
+    begun = mm(jnp.concatenate(split2(begun), axis=1), expand2)
+    grows[...] = begun
+    for c in range(NB):
+        passing[8 * c : 8 * c + 8, :] = begun[(c + 1) * BLK - 8 : (c + 1) * BLK]
+    ended = jnp.concatenate([jnp.exp(total[BLK - 1 : BLK, :] - total) for total in totals], axis=0)
+    remain[...] = mm(jnp.concatenate(split2(ended), axis=1), expand2)
+
     def masked(dy_pair):
         zero = jnp.zeros_like(dy_pair)
         return jnp.concatenate([jnp.where(low_half, dy_pair, zero), jnp.where(low_half, zero, dy_pair)], axis=0)
 
     def token_block(c, more):
         rows = block(c)
-        turned = mm(jnp.concatenate(split3(ldp[:, rows]), axis=1), lower3, NT)
-        total = turned.T
-        factors = jnp.concatenate([jnp.exp(total), jnp.exp(total[BLK - 1 : BLK, :] - total)], axis=0)
-        wide = mm(jnp.concatenate(split2(factors), axis=1), expand2)
-        grow, left = wide[:BLK], wide[BLK:]
-        remain[rows, :] = left
-        passing[pl.ds(pl.multiple_of(8 * c, 8), 8), :] = grow[BLK - 8 : BLK]
+        total, turned = totals[c], turns[c]
+        grow, left = grows[rows, :], remain[rows, :]
         dy_scaled, dy_rest = split2(dy[rows, :].astype(F32) * grow)
         dys[rows, :] = dy_scaled
         b_blk, c_blk = b_in[rows, :], c_in[rows, :]
@@ -284,7 +303,7 @@
         now16, now_rest = split2(now)
         after16[rows, :] = now16
         carried = mm(jnp.concatenate([b_blk, b_blk], axis=1), jnp.concatenate([now16, now_rest], axis=0)) * left
-        scores = mm(b_blk, c_blk, NT)
+        scores = jnp.where(causal, mm(b_blk, c_blk, NT), 0.0)
         scores2 = jnp.concatenate([scores, scores], axis=1)
         for j in range(PAIRS):
             lanes = slice(128 * j, 128 * j + 128)
@@ -299,7 +318,7 @@
                 ],
                 axis=1,
             )
-            decay = jnp.exp(jnp.where(causal2, to_row - from_col, -1e30))
+            decay = jnp.exp(jnp.minimum(to_row - from_col, 0.0))
             decays[rows, 256 * j : 256 * j + 256] = decay
             weights, weights_rest = split2(decay * scores2)
             grad_x = mm(weights, both) + mm(weights_rest, both)
@@ -338,7 +357,7 @@
     def whole_rows(i):
         rows = pl.ds(i * ROWS, ROWS)
         part = mm(feat[:, i * ROWS : (i + 1) * ROWS], gx[...], TN)
-        whole[rows, :] = part * (1.0 / TOK) + err[rows, :].astype(F32)
+        whole_hi[rows, :], whole_lo[rows, :] = split2(part * (1.0 / TOK) + err[rows, :].astype(F32))
 
     def bc_block(c, carry):
         rows = block(c)
@@ -354,7 +373,7 @@
             lanes = slice(128 * j, 128 * j + 128)
             products = mm(xin[rows, lanes], masked(dy[rows, lanes]), NT) * decays[rows, 256 * j : 256 * j + 256]
             gaps = gaps + products[:, :BLK] + products[:, BLK:]
-        gap_hi, gap_lo = split2(gaps)
+        gap_hi, gap_lo = split2(jnp.where(causal, gaps, 0.0))
         gbc[rows, 0:N] = grad_b + mm(gap_hi, c_blk) + mm(gap_lo, c_blk)
         gbc[rows, N : 2 * N] = grad_c + mm(gap_hi, b_blk, TN) + mm(gap_lo, b_blk, TN)
         return carry
@@ -375,14 +394,17 @@
         device_id_type=MESH,
     )
     swap.start()
-    first.end()
+
+    own = jnp.zeros((3 * R, COLS), F32)
+    for dy_hops in NEAR_FIRST:
+        columns = pl.ds(pl.multiple_of(first.end_part(dy_hops) * PC, 128), PC)
+        part = stack3(full_p[:, columns])
+        own = own + mm(part, whole_hi[columns, :]) + mm(part, whole_lo[columns, :])
+    local_q[:, :COLS] = fold3(own)
+    second.begin()
 
     psum = full_p[:, :D]
     parts = stack3(psum)
-    inner = fold3(mm(parts, feat[...], NT))
-    local_q[:, :COLS] = fold3(mm(parts, err[...]) + mm(stack3(inner), gx[...]) * (1.0 / TOK))
-    second.begin()
-
     cross = mm(parts, parts, NT)
     gram = jnp.zeros((R, R), F32)
     for a in range(2, -1, -1):
@@ -391,7 +413,7 @@
     inverse = inverse_factor(gram)
     second.middle()
 
-    basis = exact(inverse, psum)
+    basis = narrow(inverse, psum)
     p_out[...] = basis
     p_hi, p_lo = split2(basis * (1.0 / 128.0))
     left_out[...] = jnp.concatenate([p_hi, p_hi, p_lo, p_lo], axis=0).T
@@ -402,14 +424,14 @@
     first.settle()
     second.end()
 
-    summed = exact(inverse, full_q[:, :COLS])
+    summed = narrow(inverse, full_q[:, :COLS])
     q_out[...] = summed
     q_hi, q_lo = split2(summed)
     right_out[...] = jnp.concatenate([q_hi, q_lo, q_hi, q_lo], axis=0)
     second.settle()
 
 
-def last_kernel(whole, p_in, q_in, gbc_in, left, right, gbc_out, p_out, q_out, err_out, done, sems, out_sems):
+def last_kernel(whole_hi, whole_lo, p_in, q_in, gbc_in, left, right, gbc_out, p_out, q_out, err_out, done, sems, out_sems):
     copies = [
         pltpu.make_async_copy(gbc_in, gbc_out, sems.at[0]),
         pltpu.make_async_copy(p_in, p_out, sems.at[1]),
@@ -419,7 +441,8 @@
         copy.start()
     for i in range(D // ROWS):
         rows = pl.ds(i * ROWS, ROWS)
-        done[rows, :] = (whole[rows, :] - mm(left[rows, :], right[...])).astype(BF16)
+        whole = whole_hi[rows, :].astype(F32) + whole_lo[rows, :].astype(F32)
+        done[rows, :] = (whole - mm(left[rows, :], right[...])).astype(BF16)
         copy = pltpu.make_async_copy(done.at[rows, :], err_out.at[0, rows, :], out_sems.at[i])
         copy.start()
         copies.append(copy)
@@ -439,7 +462,8 @@
     held = pl.pallas_call(
         main_kernel,
         out_shape=(
-            VMEM((D, COLS), F32),
+            VMEM((WIDE, COLS), BF16),
+            VMEM((WIDE, COLS), BF16),
             VMEM((R, D), F32),
             VMEM((R, COLS), F32),
             VMEM((TOK, 2 * N), F32),
@@ -447,7 +471,7 @@
             VMEM((4 * R, COLS), BF16),
         ),
         in_specs=[pl.BlockSpec(memory_space=pltpu.SMEM)] + [hbm] * 8,
-        out_specs=[vm] * 6,
+        out_specs=[vm] * 7,
         scratch_shapes=[
             tokens16, tokens16, tokens16,
             VMEM((D, COLS), BF16),
@@ -456,7 +480,7 @@
             tokens16,
             VMEM((128, TOK), F32),
             VMEM((8, 128), F32), VMEM((8, COLS), F32),
-            tokens32,
+            tokens32, tokens32,
             VMEM((TOK, HEADS * BLK), F32),
             tokens16,
             VMEM((N, COLS), F32),
@@ -471,7 +495,7 @@
             dma((6, PLANE)), dma((6, PLANE)), dma((2,)), dma((6,)), dma((NB,)), dma((D // ROWS,)),
         ],
         compiler_params=pltpu.CompilerParams(
-            collective_id=0, has_side_effects=True, vmem_limit_bytes=44 * MIB
+            collective_id=0, has_side_effects=True, vmem_limit_bytes=48 * MIB
         ),
         cost_estimate=pl.CostEstimate(
             flops=2 * D * COLS * 2200, bytes_accessed=20_000_000, transcendentals=TOK * BLK * HEADS
@@ -494,7 +518,7 @@
             jax.ShapeDtypeStruct((R, COLS), F32),
             jax.ShapeDtypeStruct((1, D, COLS), BF16),
         ),
-        in_specs=[vm] * 6,
+        in_specs=[vm] * 7,
         out_specs=[hbm] * 4,
         scratch_shapes=[VMEM((D, COLS), BF16), dma((3,)), dma((D // ROWS,))],
         compiler_params=pltpu.CompilerParams(vmem_limit_bytes=16 * MIB),

time: 56.8 us -> 53.2 us (0.937)
  Pallas kernels: 55.2 us -> 51.6 us
    pallas_call x1, Pallas kernels: 53 us -> 49.5 us  [body(): pl.pallas_call(main_kernel, out_shape=(VMEM((WIDE, COLS), BF16), VMEM((WI...]
where the time goes in v4:
time: 53.2 us; the launch traced here: 53.1 us
  Pallas kernels  51.6 us (97%)
  between operations  1.45 us (3%)
    pallas_call x1, Pallas kernels, body(): pl.pallas_call(main_kernel, out_shape=(VMEM((WIDE, COLS), BF16), VMEM((WI...  49.5 us
    pallas_call x1, Pallas kernels, body(): pl.pallas_call(last_kernel, out_shape=(jax.ShapeDtypeStruct((TOK, 2 * N),...  2.15 us

profile of v4, /device:TPU:2, one launch (start us, length us, event | category | flops | bytes accessed | tf_op | source)
XLA Modules:
  0.0 53.1 jit_solution(4919438084525013952)
XLA Ops:
  1.3 49.5 %shard_map.120 = (bf16[1536,1280]{1,0:T(8,128)(2,1)S(1)}, bf16[1536,1280]{1,0:T(8,128)(2,1)S(1)}, f32[32,1280]{1,0:T(8,128)S(1)}, f32[32,1280]{1,0:T(8,128)S(1)}...) custom-call(s32[1]{0:T(128)S(6)} %copy.13.seed_ref, ...), custom_call_target="tpu_custom_call" | custom-call | flops 7208960000 | bytes 20000000 | tf_op jit(solution)/shard_map/pallas_call | solution.py:462
  50.8 2.1 %shard_map.121 = (f32[768,256]{1,0:T(8,128)}, f32[32,1280]{1,0:T(8,128)}, f32[32,1280]{1,0:T(8,128)}, bf16[1,1280,1280]{2,1,0:T(8,128)(2,1)}) custom-call(bf16[1536,1280]{1,0:T(8,128)(2,1)S(1)} %get-tuple-element.11.whole_hi, bf16[1536,1280]{1,0:T(8,128)(2,1)S(1)} %get-tuple-element.12.whole_lo, f32[32,1280]{1,0:T(8,128)S(1)} %get-tuple-element.13.p_in, ...), custom_call_target="tpu_custom_call" | custom-call | flops 419430400 | bytes 11000000 | tf_op jit(solution)/shard_map/pallas_call | solution.py:513

commit v5 on v4

--- a/solution.py
+++ b/solution.py
@@ -265,8 +265,8 @@
     causal = iota((BLK, BLK), 0) <= iota((BLK, BLK), 1)
     low_half = iota((BLK, 128), 1) < 64
 
-    for copy in small:
-        copy.wait()
+    small[0].wait()
+    small[3].wait()
     for c in range(NB - 2, -1, -1):
         dy_copy(c).start()
     for i in range(D // ROWS):
@@ -333,6 +333,8 @@
         rows = slice(low * BLK, high * BLK)
         return fold3(mm(stack3(fold3(mm(gx[rows, :], start[...]).T)), feat[rows, :]))
 
+    small[1].wait()
+    small[2].wait()
     for c in range(NB - 1, -1, -1):
         if c >= NB - 2:
             dy_copy(c).wait()
@@ -422,13 +424,13 @@
     swap.wait()
     gbc_out[...] = gbc[...] + other[...]
     first.settle()
+    second.settle()
     second.end()
 
     summed = narrow(inverse, full_q[:, :COLS])
     q_out[...] = summed
     q_hi, q_lo = split2(summed)
     right_out[...] = jnp.concatenate([q_hi, q_lo, q_hi, q_lo], axis=0)
-    second.settle()
 
 
 def last_kernel(whole_hi, whole_lo, p_in, q_in, gbc_in, left, right, gbc_out, p_out, q_out, err_out, done, sems, out_sems):

time: 53.2 us -> 53 us (level)
  no operation moved by 1% of the time
where the time goes in v5:
time: 53 us; the launch traced here: 52.9 us
  Pallas kernels  51.4 us (97%)
  between operations  1.45 us (3%)
    pallas_call x1, Pallas kernels, body(): pl.pallas_call(main_kernel, out_shape=(VMEM((WIDE, COLS), BF16), VMEM((WI...  49.3 us
    pallas_call x1, Pallas kernels, body(): pl.pallas_call(last_kernel, out_shape=(jax.ShapeDtypeStruct((TOK, 2 * N),...  2.16 us

profile of v5, /device:TPU:2, one launch (start us, length us, event | category | flops | bytes accessed | tf_op | source)
XLA Modules:
  0.0 52.9 jit_solution(2909252467871793998)
XLA Ops:
  1.3 49.3 %shard_map.120 = (bf16[1536,1280]{1,0:T(8,128)(2,1)S(1)}, bf16[1536,1280]{1,0:T(8,128)(2,1)S(1)}, f32[32,1280]{1,0:T(8,128)S(1)}, f32[32,1280]{1,0:T(8,128)S(1)}...) custom-call(s32[1]{0:T(128)S(6)} %copy.13.seed_ref, ...), custom_call_target="tpu_custom_call" | custom-call | flops 7208960000 | bytes 20000000 | tf_op jit(solution)/shard_map/pallas_call | solution.py:464
  50.5 2.2 %shard_map.121 = (f32[768,256]{1,0:T(8,128)}, f32[32,1280]{1,0:T(8,128)}, f32[32,1280]{1,0:T(8,128)}, bf16[1,1280,1280]{2,1,0:T(8,128)(2,1)}) custom-call(bf16[1536,1280]{1,0:T(8,128)(2,1)S(1)} %get-tuple-element.11.whole_hi, bf16[1536,1280]{1,0:T(8,128)(2,1)S(1)} %get-tuple-element.12.whole_lo, f32[32,1280]{1,0:T(8,128)S(1)} %get-tuple-element.13.p_in, ...), custom_call_target="tpu_custom_call" | custom-call | flops 419430400 | bytes 11000000 | tf_op jit(solution)/shard_map/pallas_call | solution.py:515
